TPU v7x, 256 devices: a whole 4x4x8 slice. The times are simulated.
256 devices in a mesh: rx: 128 (over y, x_lo, z, core), win: 2 (over x_hi).
Axes of the slice: x: 4 (x_hi: 2, x_lo: 2; x = x_hi * 2 + x_lo), y: 4, z: 8, core: 2. Of those that a mesh axis runs over, the one named last changes fastest.
Arguments:
- spectra: bfloat16 [16, 16384, 512], P('win', 'rx'), may hold values from -6 to 6
- plan: int32 [2], replicated, may hold values from 0 to 127
- mask: int32 [2, 128, 16384], P(None, 'win', 'rx'), may hold values 0 or 1
Outputs:
- stacks: bfloat16 [2, 128, 16384, 256], P(None, 'win', 'rx')
Inputs may be any that keep to these rules, and one draw needn't show every extreme that they name: plan holds rx indices.
All inputs are finite; a program needn't handle non-finite values. No bound on the sum of `mask` on one device may be relied on, other than what follows from the above.
Results may differ from a plain program's by a relative error of at most 0.0054.
Values may be sent and summed in bfloat16 or wider, within the bound.
A program may use at most 192 MiB of HBM per device.

v0:
```python
import math

import jax
import jax.numpy as jnp
from jax import lax
from jax.sharding import PartitionSpec as P

LAGS = 256
SAMPLES = 15000
BIN0 = 12


def broadcast(shard, axis, root):
    mine = lax.axis_index(axis) == root
    return lax.psum(jnp.where(mine, shard, jnp.zeros_like(shard)), axis)


def lag_table(freq, lags):
    bins = BIN0 + jnp.arange(freq, dtype=jnp.int32)
    shifts = jnp.arange(lags, dtype=jnp.int32) - lags // 2
    product = jnp.mod(bins[:, None] * shifts[None, :], SAMPLES)
    theta = 2.0 * math.pi * product.astype(jnp.float32) / SAMPLES
    scale = 1.0 / math.sqrt(freq)
    return jnp.concatenate([jnp.cos(theta) * scale, -jnp.sin(theta) * scale], 0).astype(
        jnp.bfloat16
    )


def cross_part(left, right):
    return jnp.einsum("wsf,wrf->srf", left, right, preferred_element_type=jnp.float32)


def correlate(sources, receivers, table):
    freq = table.shape[0] // 2
    count = sources.shape[0]
    sr, si = (sources[..., :freq], sources[..., freq:])
    rr, ri = (receivers[..., :freq], receivers[..., freq:])
    real = (cross_part(sr, rr) + cross_part(si, ri)) / count
    imag = (cross_part(si, rr) - cross_part(sr, ri)) / count
    stacked = jnp.concatenate([real, imag], -1).astype(jnp.bfloat16)
    flat = stacked.reshape(-1, 2 * freq)
    return jnp.dot(flat, table, preferred_element_type=jnp.float32).reshape(
        stacked.shape[0], stacked.shape[1], -1
    )


def on_device(spectra, plan, mask):
    freq = spectra.shape[2] // 2
    steps_total = plan.shape[0]
    half = mask.shape[1]
    resident = spectra.shape[1]
    table = lag_table(freq, LAGS)
    receivers = lax.all_gather(spectra, "win", axis=0, tiled=True)
    output = jnp.zeros((steps_total, half, resident, LAGS), jnp.bfloat16)
    for turn in range(steps_total):
        step = jnp.int32(turn)
        owner = plan[step]
        block = broadcast(spectra, "rx", owner)
        sources = lax.all_to_all(block, "win", split_axis=1, concat_axis=0, tiled=True)
        lagged = correlate(sources, receivers, table)
        keep = lax.dynamic_index_in_dim(mask, step, 0, keepdims=False)
        result = (lagged * keep.astype(jnp.float32)[..., None]).astype(jnp.bfloat16)
        output = lax.dynamic_update_index_in_dim(output, result, step, 0)
    return output


def solution(mesh):
    return jax.shard_map(
        on_device,
        mesh=mesh,
        in_specs=(P("win", "rx", None), P(), P(None, "win", "rx")),
        out_specs=P(None, "win", "rx", None),
        check_vma=False,
    )
```

profile of v0, /device:TPU:1, one launch (start us, length us, event | category | flops | bytes accessed | tf_op | source)
XLA Modules:
  0.0 1222.1 jit_solution(14992546963338436411)
XLA Ops:
  7.4 0.0 copy-start.5
  7.4 0.0 all-reduce.3.cloned.1.call-start
  7.4 1.3 fusion.35
  9.9 3.2 broadcast_select_fusion.1
  13.1 0.0 all-reduce.3.cloned.1.call-update
  13.2 0.0 all-gather.2.cloned.1.call-start
  13.2 2.4 copy.17
  15.6 0.0 all-gather.2.cloned.1.call-update
  15.7 1089.3 %all-reduce.3.cloned.1.call-done = (bf16[8,128,512]{2,0,1:T(8,128)(2,1)}, bf16[8,128,512]{2,0,1:T(8,128)(2,1)}) async-done(((bf16[8,128,512]{2,0,1:T(8,128)(2,1)}, bf16[8,128,512]{2,0,1:T(8,128)(2,1)}), (bf16[8,128,512]{2,0,1:T(8,128)(2,1)}, bf16[8,128,512]{2,0,1:T(8,128)(2,1)})) %all-reduce.3.cloned.1.call-update) | async-done | bytes 2097168 | tf_op jit(solution)/shard_map/psum | solution.py:15
  1105.0 13.3 %all_to_all.36 = bf16[8,128,512]{2,0,1:T(8,128)(2,1)S(1)} all-to-all(bf16[8,128,512]{2,0,1:T(8,128)(2,1)} %get-tuple-element.5), channel_id=1, replica_groups=mesh['rx'=128,'win'=2] {'win'}, dimensions={1} | all-to-all | bytes 2097152 | tf_op jit(solution)/shard_map/all_to_all | solution.py:59
  1118.3 3.6 all-to-all-start
  1121.9 0.0 copy-done.5
  1121.9 1.3 multiply_convert_fusion.7
  1123.3 1.3 copy.22
  1124.5 7.1 all-to-all-done
  1131.6 0.3 copy.15
  1132.0 0.1 fusion.33
  1132.1 1.0 copy.28
  1133.0 1.3 fusion.34
  1134.3 1.9 copy.30
  1136.2 1.9 copy.29
  1138.1 1.9 copy.31
  1140.0 0.0 all-gather.2.cloned.1.call-done
  1140.0 0.0 copy-start
  1140.0 0.0 copy-start.2
  1140.0 3.1 fusion.18
  1143.0 0.0 copy-done
  1143.1 0.0 copy-done.2
  1143.1 1.4 fusion.20
  1144.4 0.0 copy-start.3
  1144.5 3.7 fusion.8
  1148.2 0.0 copy-done.3
  1148.2 3.7 fusion.7
  1151.9 7.6 pad_maximum_fusion.1
  1159.5 2.6 fusion.22
  1162.1 1.6 fusion.24
  1163.7 0.0 copy-start.1
  1163.7 3.7 fusion.5
  1167.4 0.0 copy-done.1
  1167.4 3.7 fusion.4
  1171.1 7.4 pad_maximum_fusion
  1178.5 0.0 copy-start.4
  1178.5 8.9 fusion.9
  1187.4 0.0 copy-done.4
  1187.4 20.9 %fusion.6 = bf16[1,64,128,256]{3,2,1,0:T(8,128)(2,1)} fusion(f32[64,128]{1,0:T(8,128)S(1)} %get-tuple-element.13, bf16[64,128,512]{1,0,2:T(8,128)(2,1)S(1)} %copy-done.4, bf16[256,256]{1,0:T(8,128)(2,1)S(1)} %get-tuple-element.16, bf16[256,256]{1,0:T(8,128)(2,1)S(1)} %get-tuple-element.15), kind=kOutput, calls=%fused_computation.15 | convolution fusion | flops 2152202240 | bytes 12877824 | tf_op jit(solution)/shard_map/dot_general | solution.py:42
  1208.3 6.3 pad_maximum_fusion.2
  (2 shorter events, 0.0 us)
Async XLA Ops:
  7.4 1114.5 %copy-start.5 = (s32[2,64,128]{2,1,0:T(8,128)S(1)}, s32[2,64,128]{2,1,0:T(8,128)}, u32[]{:S(2)}) copy-start(s32[2,64,128]{2,1,0:T(8,128)} %param.5) | copy-start | bytes 196612
  7.4 1097.6 %all-reduce.3.cloned.1.call-start = ((), (), s32[]{:S(2)}) async-start(), calls=%async_computation.3 | async-start | bytes 4194304 | tf_op jit(solution)/shard_map/psum | solution.py:15
  13.2 1126.8 %all-gather.2.cloned.1.call-start = ((), (), s32[]{:S(2)}) async-start(), calls=%async_computation.2 | async-start | bytes 3145728 | tf_op jit(solution)/shard_map/all_gather | solution.py:53
  1118.3 13.3 %all-to-all-start = ((bf16[8,128,512]{2,0,1:T(8,128)(2,1)}), bf16[8,128,512]{2,0,1:T(8,128)(2,1)S(1)}, u32[]{:S(2)}, u32[]{:S(2)}) async-start(bf16[8,128,512]{2,0,1:T(8,128)(2,1)} %get-tuple-element.6), calls=%async_computation | async-start | bytes 2097152 | tf_op jit(solution)/shard_map/all_to_all | solution.py:59
  1140.0 3.1 copy-start
  1140.0 3.1 copy-start.2
  1144.4 3.7 copy-start.3
  1163.7 3.7 copy-start.1
  1178.5 8.9 copy-start.4
Sparse Core Ops, SparseCore 0:
  13.3 1091.6 all-reduce.2
Sparse Core Ops, SparseCore 1:
  15.8 43.8 all-gather.1
where the time goes:
time: 1230 us; the launch traced here: 1220 us
  waiting for transfers between devices  1100 us (89%)
  matrix products  53.2 us (4%)
  other arithmetic  25.9 us (2%)
  between operations  16.2 us (1%)
  local copies, waits for them, and re-layouts  13.4 us (1%)
  blocking collectives  13.3 us (1%)
    psum x1, waiting for transfers between devices, broadcast(): return lax.psum(jnp.where(mine, shard, jnp.zeros_like(shard)), axis)  1090 us
    dot_general x2, matrix products, correlate(): jnp.dot(flat, table, preferred_element_type=jnp.float32)  29.8 us
  transfers between devices with their start and end apart: 3, of which 2 were waited for; matrix products, arithmetic and copies ran while one was open for 1% of the time, Pallas kernels for 0%

commit v1 on v0

v1 whole, which is shorter than its diff:
```python
import math

import jax
import jax.numpy as jnp
import numpy as np
from jax import lax
from jax.experimental import pallas as pl
from jax.experimental.pallas import tpu as pltpu
from jax.sharding import PartitionSpec as P

LAGS = 256
SAMPLES = 15000
BIN0 = 12
NF = 256
WINDOWS = 16
CH = 128
HALF = 64
GROUPS = 32
MESH = pl.DeviceIdType.MESH
NY, NZ = 4, 8
BATCH = 8
BUFFERS = 2 * BATCH


def table_transposed():
    bins = BIN0 + np.arange(NF)
    shifts = np.arange(LAGS) - LAGS // 2
    theta = 2.0 * math.pi * np.mod(bins[:, None] * shifts[None, :], SAMPLES) / SAMPLES
    scale = 1.0 / math.sqrt(NF)
    table = np.concatenate([np.cos(theta) * scale, -np.sin(theta) * scale], 0)
    table = table.astype(np.float32).astype(jnp.bfloat16).astype(np.float32)
    return np.ascontiguousarray((table / WINDOWS).T).astype(jnp.bfloat16)


def owner_of(plan_ref, block):
    rx = plan_ref[block]
    return rx // 32, (rx // 16) % 2, (rx // 2) % NZ, rx % 2


def spread_kernel(
    plan_ref, spec_ref, cross,
    near, far, from_y, relay_p, relay_m, to_core, from_core, to_z, from_z, relay_z, to_x, from_x,
    gathered, transit_p, transit_m, weights, sources,
    in_sem, y_send, y_recv, relay_sems, core_sems, z_send, z_recv, zr_sems, x_send, x_recv,
    gy_send, gy_recv, ring_send, ring_recv, gc_send, gc_recv,
    hop1_send, hop1_recv, hop2_send, hop2_recv,
):
    rx, win = lax.axis_index("rx"), lax.axis_index("win")
    core, z, x_lo, y = rx % 2, (rx // 2) % NZ, (rx // 16) % 2, rx // 32

    def at(y_=y, x_=x_lo, z_=z, core_=core, win_=win):
        return {"rx": ((y_ * 2 + x_) * NZ + z_) * 2 + core_, "win": win_}

    def remote(src, dst, send, recv, device):
        return pltpu.make_async_remote_copy(
            src_ref=src, dst_ref=dst, send_sem=send, recv_sem=recv, device_id=device, device_id_type=MESH
        )

    def arrived(ref, recv):
        remote(ref, ref, recv, recv, at()).wait_recv()

    load = pltpu.make_async_copy(spec_ref, near, in_sem)
    load.start()

    plus = at(x_=1 - x_lo, win_=(win + x_lo) % 2)
    minus = at(x_=1 - x_lo, win_=(win + 1 - x_lo) % 2)
    ys = [(y + d) % NY for d in range(1, NY)]
    zs = [(z + d) % NZ for d in range(1, NZ)]
    peers = [at(y_=v) for v in ys] + [at(z_=v) for v in zs] + [at(core_=1 - core)]
    peers += [plus, minus, at(win_=1 - win)]
    barrier = pltpu.get_barrier_semaphore()
    for peer in peers:
        pl.semaphore_signal(barrier, inc=1, device_id=peer, device_id_type=MESH)
    pl.semaphore_wait(barrier, len(peers))

    sent = []

    def go(copy):
        copy.start()
        sent.append(copy)

    next_y, across, last_y = ys
    go(remote(spec_ref.at[0:4, :, across], relay_p, relay_sems.at[0], relay_sems.at[1], at(y_=next_y)))
    go(remote(spec_ref.at[4:8, :, across], relay_m, relay_sems.at[2], relay_sems.at[3], at(y_=last_y)))
    go(remote(spec_ref.at[:, :, next_y], from_y.at[y], y_send.at[0], y_recv.at[0], at(y_=next_y)))
    go(remote(spec_ref.at[:, :, last_y], from_y.at[y], y_send.at[1], y_recv.at[1], at(y_=last_y)))
    for i in range(4):
        go(remote(spec_ref.at[i], transit_p.at[i], hop1_send.at[i], hop1_recv.at[i], plus))
        go(remote(spec_ref.at[4 + i], transit_m.at[i], hop1_send.at[4 + i], hop1_recv.at[4 + i], minus))

    def window_pair(ref, side):
        def body(i, carry):
            both = [
                ref[2 * i + k].reshape(CH, 2 * NF).astype(jnp.float32).T.reshape(2, GROUPS, 8, CH) for k in range(2)
            ]
            a = jnp.concatenate([both[0][0], both[1][0]], 1).astype(jnp.bfloat16)
            b = jnp.concatenate([both[0][1], both[1][1]], 1)
            minus_b = (-b).astype(jnp.bfloat16)
            b = b.astype(jnp.bfloat16)
            row = pl.multiple_of(side * CH + 16 * i, 16)
            weights[:, pl.ds(row, 16), :CH] = a
            weights[:, pl.ds(HALF + row, 16), :CH] = b
            weights[:, pl.ds(row, 16), CH:] = minus_b
            weights[:, pl.ds(HALF + row, 16), CH:] = a
            return carry

        lax.fori_loop(0, 4, body, 0)

    load.wait()
    from_y[y] = near[:, :, y]
    arrived(relay_p, relay_sems.at[1])
    go(remote(relay_p, from_y.at[last_y, 0:4], relay_sems.at[4], y_recv.at[2], at(y_=next_y)))
    arrived(relay_m, relay_sems.at[3])
    go(remote(relay_m, from_y.at[next_y, 4:8], relay_sems.at[5], y_recv.at[3], at(y_=last_y)))
    window_pair(near, win)

    arrived(from_y.at[last_y], y_recv.at[0])
    arrived(from_y.at[next_y], y_recv.at[1])
    arrived(from_y.at[across, 0:4], y_recv.at[2])
    arrived(from_y.at[across, 4:8], y_recv.at[3])
    for b in range(2):
        oy = owner_of(plan_ref, b)[0]
        to_core[b] = from_y[oy, :, 1 - core]
        from_core[core, b] = from_y[oy, :, core]

    go(remote(to_core, from_core.at[core], core_sems.at[0], core_sems.at[1], at(core_=1 - core)))
    for i in range(4):
        arrived(transit_p.at[i], hop1_recv.at[i])
        go(remote(transit_p.at[i], far.at[i], hop2_send.at[i], hop2_recv.at[i], plus))
        arrived(transit_m.at[i], hop1_recv.at[4 + i])
        go(remote(transit_m.at[i], far.at[4 + i], hop2_send.at[4 + i], hop2_recv.at[4 + i], minus))
    arrived(from_core.at[1 - core], core_sems.at[1])
    for b in range(2):
        picked = from_core[owner_of(plan_ref, b)[3], b].astype(jnp.float32)
        picked = jnp.transpose(picked, (1, 0, 2))
        picked = jnp.concatenate([picked[:, :, :NF], picked[:, :, NF:]], 1)
        to_z[:, b] = picked.astype(jnp.bfloat16).reshape(NZ, 2, 16, NF)

    opposite, three_down, one_down = zs[3], zs[4], zs[6]
    go(remote(to_z.at[opposite, :, 1], relay_z, zr_sems.at[0], zr_sems.at[1], at(z_=three_down)))
    go(remote(to_z.at[opposite, :, 0], from_z.at[z, :, 0], z_send.at[3], z_recv.at[z], at(z_=opposite)))
    for d, v in enumerate(zs):
        if d != 3:
            go(remote(to_z.at[v], from_z.at[z], z_send.at[d], z_recv.at[z], at(z_=v)))
    from_z[z] = to_z[z]

    shape = (GROUPS * 16, NF)
    pick_group = (lax.broadcasted_iota(jnp.int32, shape, 1) >> 3) == (lax.broadcasted_iota(jnp.int32, shape, 0) >> 4)
    shape = (GROUPS * 16, CH)
    pick_row = (lax.broadcasted_iota(jnp.int32, shape, 1) >> 3) == (lax.broadcasted_iota(jnp.int32, shape, 0) & 15)
    f = lax.broadcasted_iota(jnp.int32, (NF, CH), 0)
    n = lax.broadcasted_iota(jnp.int32, (NF, CH), 1)
    same_place = ((f & 7) == (n & 7)).astype(jnp.float32).astype(jnp.bfloat16)
    out_row = lax.broadcasted_iota(jnp.int32, (GROUPS, GROUPS * 16), 0)
    in_row = lax.broadcasted_iota(jnp.int32, (GROUPS, GROUPS * 16), 1)
    same_group = ((in_row >> 4) == out_row).astype(jnp.float32).astype(jnp.bfloat16)

    arrived(relay_z, zr_sems.at[1])
    go(remote(relay_z, from_z.at[zs[2], :, 1], zr_sems.at[2], zr_sems.at[3], at(z_=one_down)))
    for d, v in enumerate(zs):
        if d != 3:
            arrived(from_z.at[v], z_recv.at[v])
    arrived(from_z.at[opposite, :, 0], z_recv.at[opposite])
    arrived(from_z.at[opposite, :, 1], zr_sems.at[3])

    def regroup(i, carry):
        b, e = i // 2, i % 2
        rows = from_z[owner_of(plan_ref, b)[2], b, e].astype(jnp.float32).reshape(1, 16, NF)
        rows = jnp.broadcast_to(rows, (GROUPS, 16, NF)).reshape(GROUPS * 16, NF)
        rows = jnp.where(pick_group, rows, 0.0).astype(jnp.bfloat16)
        moved = jnp.dot(rows, same_place, preferred_element_type=jnp.float32)
        moved = jnp.where(pick_row, moved, 0.0).astype(jnp.bfloat16)
        done = jnp.dot(same_group, moved, preferred_element_type=jnp.float32)
        to_x[b, e] = done.astype(jnp.bfloat16)
        return carry

    lax.fori_loop(0, 4, regroup, 0, unroll=2)

    active = win == core
    there = from_x.at[x_lo, win]
    go(remote(to_x, there, x_send.at[0], x_recv.at[x_lo, win], at(x_=1 - x_lo, win_=core)))

    def over():
        return remote(to_x, there, x_send.at[1], x_recv.at[x_lo, win], at(win_=core))

    @pl.when(win != core)
    def _():
        over().start()

    own = gathered.at[z, y]

    def over_y():
        return [remote(own, own, gy_send.at[d], gy_recv.at[y], at(y_=v)) for d, v in enumerate(ys)]

    @pl.when(active)
    def _():
        from_x[x_lo, win] = to_x[...]
        arrived(from_x.at[1 - x_lo, win], x_recv.at[1 - x_lo, win])
        arrived(from_x.at[0, 1 - win], x_recv.at[0, 1 - win])
        arrived(from_x.at[1, 1 - win], x_recv.at[1, 1 - win])

        for b in range(2):
            ox = owner_of(plan_ref, b)[1]
            for w in range(2):
                gathered[z, y, b, :, :, w * CH : (w + 1) * CH] = from_x[ox, w, b]
        for copy in over_y():
            copy.start()

    for i in range(8):
        arrived(far.at[i], hop2_recv.at[i])
    window_pair(far, 1 - win)

    lane = lax.broadcasted_iota(jnp.int32, (1, 8, 2 * CH), 2)
    sub = lax.broadcasted_iota(jnp.int32, (1, 8, 2 * CH), 1)
    diagonal = (lane & 7) == sub

    def correlate(slots):
        count = len(slots)

        def unpack(v, carry):
            for i, slot in enumerate(slots):
                sources[i, v] = gathered[slot, v].astype(jnp.float32)
            return carry

        lax.fori_loop(0, NY, unpack, 0)

        def product(g):
            row = sources[:count, :, :, :, pl.ds(g, 1), :].reshape(count * 16, 1, 2 * CH)
            spread = jnp.where(diagonal, row, 0.0)
            spread = spread.reshape(count * 16 * 8, 2 * CH).astype(jnp.bfloat16)
            res = jnp.dot(spread, weights[g], preferred_element_type=jnp.float32)
            return res.reshape(count * 16, 8, 2 * CH)

        def bins(gg, carry):
            res = jnp.concatenate([product(2 * gg), product(2 * gg + 1)], 1)
            res = res.astype(jnp.bfloat16).reshape(count, NY, 2, 2, 16, 2 * CH)
            row = pl.multiple_of(gg * 16, 16)
            for i, slot in enumerate(slots):
                for b in range(2):
                    for c in range(2):
                        for s in range(2):
                            cross[b, :, slot, pl.ds(c * NF + row, 16), s * CH : (s + 1) * CH] = res[
                                i, :, b, s, :, c * CH : (c + 1) * CH
                            ]
            return carry

        lax.fori_loop(0, GROUPS // 2, bins, 0, unroll=2)

    def down(t):
        return (z + NZ - t) % NZ

    def up(t):
        return (z + t) % NZ

    def pieces(t):
        return [(0, 0), (1, 1)] if t == 3 else [(0, 0), (1, 0), (0, 1), (1, 1)]

    def ring_piece(t, way, half):
        ref = gathered.at[down(t) if way == 0 else up(t), 2 * half : 2 * half + 2]
        return remote(
            ref, ref, ring_send.at[way, t, half], ring_recv.at[way, t, half], at(z_=up(1) if way == 0 else down(1))
        )

    def ring_arrived(t, way, half):
        ref = gathered.at[down(t) if way == 0 else up(t), 2 * half : 2 * half + 2]
        arrived(ref, ring_recv.at[way, t - 1, half])

    def pass_on(slot):
        ref = gathered.at[slot]
        return remote(ref, ref, gc_send.at[slot], gc_recv.at[slot], at(core_=1 - core))

    slots = [[z], [down(1), up(1)], [down(2), up(2)], [down(3), up(3)], [up(4)]]
    done = []
    for t in range(5):

        @pl.when(active)
        def _():
            if t == 0:
                for v in ys:
                    arrived(gathered.at[z, v], gy_recv.at[v])
                for way, half in pieces(0):
                    ring_piece(0, way, half).start()
            else:
                for way, half in pieces(t - 1):
                    ring_arrived(t, way, half)
                    if t < 4 and (way, half) in pieces(t):
                        ring_piece(t, way, half).start()
            for slot in slots[t]:
                pass_on(slot).start()

        @pl.when(win != core)
        def _():
            for slot in slots[t]:
                arrived(gathered.at[slot], gc_recv.at[slot])

        correlate(slots[t])
        done.extend(slots[t])

    for copy in sent:
        copy.wait_send()

    @pl.when(win != core)
    def _():
        over().wait_send()

    @pl.when(active)
    def _():
        for copy in over_y() + [pass_on(slot) for slot in done]:
            copy.wait_send()
        for t in range(4):
            for way, half in pieces(t):
                ring_piece(t, way, half).wait_send()


def spread(plan, spectra):
    bf = jnp.bfloat16
    piece = (2, 16, NF)
    dma = pltpu.SemaphoreType.DMA
    natural = (2, NY, 16, 2 * NF)
    return pl.pallas_call(
        spread_kernel,
        out_shape=jax.ShapeDtypeStruct((2, NY, NZ, 2 * NF, 2 * CH), bf),
        in_specs=[pl.BlockSpec(memory_space=pltpu.SMEM), pl.BlockSpec(memory_space=pltpu.HBM)],
        out_specs=pl.BlockSpec(memory_space=pltpu.VMEM),
        scratch_shapes=[
            pltpu.VMEM((8,) + natural, bf),
            pltpu.VMEM((8,) + natural, bf),
            pltpu.VMEM((NY, 8, 2, 16, 2 * NF), bf),
            pltpu.VMEM((4, 2, 16, 2 * NF), bf),
            pltpu.VMEM((4, 2, 16, 2 * NF), bf),
            pltpu.VMEM((2, 8, 16, 2 * NF), bf),
            pltpu.VMEM((2, 2, 8, 16, 2 * NF), bf),
            pltpu.VMEM((NZ, 2) + piece, bf),
            pltpu.VMEM((NZ, 2) + piece, bf),
            pltpu.VMEM(piece, bf),
            pltpu.VMEM((2, 2, GROUPS, CH), bf),
            pltpu.VMEM((2, 2, 2, 2, GROUPS, CH), bf),
            pltpu.VMEM((NZ, NY, 2, 2, GROUPS, 2 * CH), bf),
            pltpu.VMEM((4,) + natural, bf),
            pltpu.VMEM((4,) + natural, bf),
            pltpu.VMEM((GROUPS, 2 * CH, 2 * CH), bf),
            pltpu.VMEM((2, NY, 2, 2, GROUPS, 2 * CH), jnp.float32),
            dma, dma((2,)), dma((4,)), dma((6,)), dma((2,)), dma((7,)), dma((NZ,)), dma((4,)), dma((2,)), dma((2, 2)),
            dma((3,)), dma((NY,)), dma((2, 4, 2)), dma((2, 4, 2)), dma((NZ,)), dma((NZ,)),
            dma((8,)), dma((8,)), dma((8,)), dma((8,)),
        ],
        compiler_params=pltpu.CompilerParams(
            collective_id=0, has_side_effects=True, vmem_limit_bytes=28 * 1024 * 1024
        ),
    )(plan, spectra.reshape((8,) + natural))


def lag_kernel(cross, mask_ref, table_ref, out_ref, stage, out_sems):
    half = HALF // 2

    def result(p):
        slot = lax.rem(p, BUFFERS)
        place = out_ref.at[p // half, pl.ds(2 * lax.rem(p, half), 2)]
        return pltpu.make_async_copy(stage.at[slot], place, out_sems.at[slot])

    def batch(i, drain):
        pairs = [BATCH * i + k for k in range(BATCH)]
        if drain:
            for p in pairs:
                result(p - BUFFERS).wait()
        for p in pairs:
            b, row = p // half, 2 * lax.rem(p, half)
            lagged = jnp.dot(table_ref[...], cross[b, lax.rem(p, half)], preferred_element_type=jnp.float32)
            for s in range(2):
                keep = mask_ref[b, pl.ds(row + s, 1), :].astype(jnp.float32)
                kept = (lagged[:, s * CH : (s + 1) * CH] * keep).astype(jnp.bfloat16)
                stage[lax.rem(p, BUFFERS), s] = kept.T
        for p in pairs:
            result(p).start()

    def first(i, carry):
        batch(i, False)
        return carry

    def rest(i, carry):
        batch(i, True)
        return carry

    lax.fori_loop(0, 2, first, 0)
    lax.fori_loop(2, HALF // BATCH, rest, 0)
    for k in range(BUFFERS):
        result(HALF - BUFFERS + k).wait()


def lags(cross, mask):
    vmem = pl.BlockSpec(memory_space=pltpu.VMEM)
    return pl.pallas_call(
        lag_kernel,
        out_shape=jax.ShapeDtypeStruct((2, HALF, CH, LAGS), jnp.bfloat16),
        in_specs=[vmem, vmem, vmem],
        out_specs=pl.BlockSpec(memory_space=pltpu.HBM),
        scratch_shapes=[
            pltpu.VMEM((BUFFERS, 2, CH, LAGS), jnp.bfloat16),
            pltpu.SemaphoreType.DMA((BUFFERS,)),
        ],
        compiler_params=pltpu.CompilerParams(vmem_limit_bytes=28 * 1024 * 1024),
    )(cross.reshape(2, HALF // 2, 2 * NF, 2 * CH), mask, jnp.asarray(table_transposed()))


def on_device(spectra, plan, mask):
    return lags(spread(plan, spectra), mask)


def solution(mesh):
    return jax.shard_map(
        on_device,
        mesh=mesh,
        in_specs=(P("win", "rx", None), P(), P(None, "win", "rx")),
        out_specs=P(None, "win", "rx", None),
        check_vma=False,
    )
```

time: 1230 us -> 76.3 us (0.06)
  waiting for transfers between devices: 1100 us -> 0 us
  Pallas kernels: 0 us -> 74.3 us
  matrix products: 53.2 us -> 0 us
  other arithmetic: 25.9 us -> 0 us
  between operations: 16.2 us -> 0.03 us
  blocking collectives: 13.3 us -> 0 us
    psum x1 -> x0, waiting for transfers between devices: 1090 us -> none  [broadcast(): return lax.psum(jnp.where(mine, shard, jnp.zeros_like(shard)), axis)]
    pallas_call x0 -> x2, Pallas kernels: none -> 74.3 us  [the longest x1 66.2 us: spread(): pl.pallas_call(spread_kernel, out_shape=jax.ShapeDtypeStruct((2, NY, NZ,...]
    dot_general x10 -> x0, matrix products: 53.2 us -> none  [the longest x2 29.8 us: correlate(): jnp.dot(flat, table, preferred_element_type=jnp.float32)]
    concatenate x2 -> x0, other arithmetic: 15 us -> none  [correlate(): stacked = jnp.concatenate([real, imag], -1).astype(jnp.bfloat16)]
    all_to_all x1 -> x0, blocking collectives: 13.3 us -> none  [on_device(): lax.all_to_all(block, 'win', split_axis=1, concat_axis=0, tiled=True)]
  transfers between devices with their start and end apart: 3 -> 0, of which waited for: 2 -> 0; matrix products, arithmetic and copies ran while one was open for 1% -> 0% of each run, Pallas kernels for 0% -> 0%
where the time goes in v1:
time: 76.3 us; the launch traced here: 76.2 us
  Pallas kernels  74.3 us (97%)
  local copies, waits for them, and re-layouts  1.89 us (2%)
    pallas_call x1, Pallas kernels, spread(): pl.pallas_call(spread_kernel, out_shape=jax.ShapeDtypeStruct((2, NY, NZ,...  66.2 us
    pallas_call x1, Pallas kernels, lags(): pl.pallas_call(lag_kernel, out_shape=jax.ShapeDtypeStruct((2, HALF, CH, L...  8.06 us
    unnamed x8, local copies, waits for them, and re-layouts  1.89 us

profile of v1, /device:TPU:1, one launch (start us, length us, event | category | flops | bytes accessed | tf_op | source)
XLA Modules:
  0.0 76.2 jit_solution(17249647333592548996)
XLA Ops:
  0.0 0.0 copy-start
  0.0 1.2 %copy-done = bf16[8,128,512]{2,1,0:T(8,128)(2,1)S(1)} copy-done((bf16[8,128,512]{2,1,0:T(8,128)(2,1)S(1)}, bf16[8,128,512]{2,1,0:T(8,128)(2,1)}, u32[]{:S(2)}) %copy-start) | copy-done | bytes 1048600
  1.2 0.0 copy-start.3
  1.2 0.7 copy-done.3
  1.9 0.0 copy-start.1
  1.9 0.0 copy-start.2
  1.9 66.2 %shard_map.46 = bf16[2,4,8,512,256]{4,3,2,1,0:T(8,128)(2,1)S(1)} custom-call(s32[2]{0:T(128)S(1)} %copy-done.3, bf16[8,2,4,16,512]{4,3,2,1,0:T(8,128)(2,1)S(1)} %bitcast.3), custom_call_target="tpu_custom_call" | custom-call | tf_op jit(solution)/shard_map/pallas_call | solution.py:320
  68.1 0.0 copy-done.1
  68.1 0.0 copy-done.2
  68.1 8.1 %shard_map.47 = bf16[2,64,128,256]{3,2,1,0:T(8,128)(2,1)} custom-call(bf16[2,32,512,256]{3,2,1,0:T(8,128)(2,1)S(1)} %bitcast.2, s32[2,64,128]{2,1,0:T(8,128)S(1)} %copy-done.2, bf16[256,512]{1,0:T(8,128)(2,1)S(1)} %copy-done.1), custom_call_target="tpu_custom_call" | custom-call | tf_op jit(solution)/shard_map/pallas_call | solution.py:392
Async XLA Ops:
  0.0 1.2 %copy-start = (bf16[8,128,512]{2,1,0:T(8,128)(2,1)S(1)}, bf16[8,128,512]{2,1,0:T(8,128)(2,1)}, u32[]{:S(2)}) copy-start(bf16[8,128,512]{2,1,0:T(8,128)(2,1)} %param.4) | copy-start | bytes 3145732
  1.2 0.7 copy-start.3
  1.9 66.2 %copy-start.1 = (bf16[256,512]{1,0:T(8,128)(2,1)S(1)}, bf16[256,512]{1,0:T(8,128)(2,1)}, u32[]{:S(2)}) copy-start(bf16[256,512]{1,0:T(8,128)(2,1)} %constant.2.clone.table_ref) | copy-start | bytes 786436
  1.9 66.2 %copy-start.2 = (s32[2,64,128]{2,1,0:T(8,128)S(1)}, s32[2,64,128]{2,1,0:T(8,128)}, u32[]{:S(2)}) copy-start(s32[2,64,128]{2,1,0:T(8,128)} %mask_ref.1) | copy-start | bytes 196612

commit v2 on v1

--- a/solution.py
+++ b/solution.py
@@ -18,7 +18,7 @@
 GROUPS = 32
 MESH = pl.DeviceIdType.MESH
 NY, NZ = 4, 8
-BATCH = 8
+BATCH = 16
 BUFFERS = 2 * BATCH
 
 
@@ -38,11 +38,11 @@
 
 
 def spread_kernel(
-    plan_ref, spec_ref, cross,
-    near, far, from_y, relay_p, relay_m, to_core, from_core, to_z, from_z, relay_z, to_x, from_x,
+    plan_hbm, spec_ref, cross,
+    plan_ref, near, far, from_y, relay_p, relay_m, to_core, from_core, to_z, from_z, relay_z, to_x, from_x,
     gathered, transit_p, transit_m, weights, sources,
-    in_sem, y_send, y_recv, relay_sems, core_sems, z_send, z_recv, zr_sems, x_send, x_recv,
-    gy_send, gy_recv, ring_send, ring_recv, gc_send, gc_recv,
+    y_send, y_recv, relay_sems, core_sems, z_send, z_recv, zr_sems, x_send, x_recv,
+    gy_send, gy_recv, ring_send, ring_recv, gc_send, gc_recv, last_send, last_recv, in_sems,
     hop1_send, hop1_recv, hop2_send, hop2_recv,
 ):
     rx, win = lax.axis_index("rx"), lax.axis_index("win")
@@ -59,8 +59,13 @@
     def arrived(ref, recv):
         remote(ref, ref, recv, recv, at()).wait_recv()
 
-    load = pltpu.make_async_copy(spec_ref, near, in_sem)
-    load.start()
+
+    loads = [
+        pltpu.make_async_copy(spec_ref, near, in_sems.at[0]),
+        pltpu.make_async_copy(plan_hbm, plan_ref, in_sems.at[1]),
+    ]
+    for load in loads:
+        load.start()
 
     plus = at(x_=1 - x_lo, win_=(win + x_lo) % 2)
     minus = at(x_=1 - x_lo, win_=(win + 1 - x_lo) % 2)
@@ -106,7 +111,8 @@
 
         lax.fori_loop(0, 4, body, 0)
 
-    load.wait()
+    for load in loads:
+        load.wait()
     from_y[y] = near[:, :, y]
     arrived(relay_p, relay_sems.at[1])
     go(remote(relay_p, from_y.at[last_y, 0:4], relay_sems.at[4], y_recv.at[2], at(y_=next_y)))
@@ -124,11 +130,14 @@
         from_core[core, b] = from_y[oy, :, core]
 
     go(remote(to_core, from_core.at[core], core_sems.at[0], core_sems.at[1], at(core_=1 - core)))
-    for i in range(4):
+    def forward(i):
         arrived(transit_p.at[i], hop1_recv.at[i])
         go(remote(transit_p.at[i], far.at[i], hop2_send.at[i], hop2_recv.at[i], plus))
         arrived(transit_m.at[i], hop1_recv.at[4 + i])
         go(remote(transit_m.at[i], far.at[4 + i], hop2_send.at[4 + i], hop2_recv.at[4 + i], minus))
+
+    for i in range(3):
+        forward(i)
     arrived(from_core.at[1 - core], core_sems.at[1])
     for b in range(2):
         picked = from_core[owner_of(plan_ref, b)[3], b].astype(jnp.float32)
@@ -143,6 +152,7 @@
         if d != 3:
             go(remote(to_z.at[v], from_z.at[z], z_send.at[d], z_recv.at[z], at(z_=v)))
     from_z[z] = to_z[z]
+    forward(3)
 
     shape = (GROUPS * 16, NF)
     pick_group = (lax.broadcasted_iota(jnp.int32, shape, 1) >> 3) == (lax.broadcasted_iota(jnp.int32, shape, 0) >> 4)
@@ -214,7 +224,7 @@
     sub = lax.broadcasted_iota(jnp.int32, (1, 8, 2 * CH), 1)
     diagonal = (lane & 7) == sub
 
-    def correlate(slots):
+    def correlate(slots, part=None):
         count = len(slots)
 
         def unpack(v, carry):
@@ -222,7 +232,8 @@
                 sources[i, v] = gathered[slot, v].astype(jnp.float32)
             return carry
 
-        lax.fori_loop(0, NY, unpack, 0)
+        if part != 1:
+            lax.fori_loop(0, NY, unpack, 0)
 
         def product(g):
             row = sources[:count, :, :, :, pl.ds(g, 1), :].reshape(count * 16, 1, 2 * CH)
@@ -244,7 +255,8 @@
                             ]
             return carry
 
-        lax.fori_loop(0, GROUPS // 2, bins, 0, unroll=2)
+        quarter = GROUPS // 4
+        lax.fori_loop(quarter if part == 1 else 0, quarter if part == 0 else 2 * quarter, bins, 0, unroll=4)
 
     def down(t):
         return (z + NZ - t) % NZ
@@ -269,8 +281,21 @@
         ref = gathered.at[slot]
         return remote(ref, ref, gc_send.at[slot], gc_recv.at[slot], at(core_=1 - core))
 
+    def pass_last(half):
+        ref = gathered.at[up(4), 2 * half : 2 * half + 2]
+        return remote(ref, ref, last_send.at[half], last_recv.at[half], at(core_=1 - core))
+
+    def receive(t, late):
+        ways = ([(0, 0)], [(1, 1)]) if t == 4 else ([(0, 0), (1, 0)], [(0, 1), (1, 1)])
+        for way, half in ways[late]:
+            ring_arrived(t, way, half)
+            if t == 4:
+                pass_last(half).start()
+            elif (way, half) in pieces(t):
+                ring_piece(t, way, half).start()
+
     slots = [[z], [down(1), up(1)], [down(2), up(2)], [down(3), up(3)], [up(4)]]
-    done = []
+    done = sum(slots, [])
     for t in range(5):
 
         @pl.when(active)
@@ -281,20 +306,32 @@
                 for way, half in pieces(0):
                     ring_piece(0, way, half).start()
             else:
-                for way, half in pieces(t - 1):
-                    ring_arrived(t, way, half)
-                    if t < 4 and (way, half) in pieces(t):
-                        ring_piece(t, way, half).start()
-            for slot in slots[t]:
-                pass_on(slot).start()
+                if t == 1:
+                    receive(t, 0)
+                receive(t, 1)
+            if t < 4:
+                for slot in slots[t]:
+                    pass_on(slot).start()
 
         @pl.when(win != core)
         def _():
-            for slot in slots[t]:
-                arrived(gathered.at[slot], gc_recv.at[slot])
-
-        correlate(slots[t])
-        done.extend(slots[t])
+            if t < 4:
+                for slot in slots[t]:
+                    arrived(gathered.at[slot], gc_recv.at[slot])
+            else:
+                for half in range(2):
+                    arrived(gathered.at[up(4), 2 * half : 2 * half + 2], last_recv.at[half])
+
+        if 0 < t < 4:
+            correlate(slots[t], 0)
+
+            @pl.when(active)
+            def _():
+                receive(t + 1, 0)
+
+            correlate(slots[t], 1)
+        else:
+            correlate(slots[t])
 
     for copy in sent:
         copy.wait_send()
@@ -305,7 +342,7 @@
 
     @pl.when(active)
     def _():
-        for copy in over_y() + [pass_on(slot) for slot in done]:
+        for copy in over_y() + [pass_on(slot) for slot in done[:7]] + [pass_last(half) for half in range(2)]:
             copy.wait_send()
         for t in range(4):
             for way, half in pieces(t):
@@ -320,9 +357,10 @@
     return pl.pallas_call(
         spread_kernel,
         out_shape=jax.ShapeDtypeStruct((2, NY, NZ, 2 * NF, 2 * CH), bf),
-        in_specs=[pl.BlockSpec(memory_space=pltpu.SMEM), pl.BlockSpec(memory_space=pltpu.HBM)],
+        in_specs=[pl.BlockSpec(memory_space=pltpu.HBM), pl.BlockSpec(memory_space=pltpu.HBM)],
         out_specs=pl.BlockSpec(memory_space=pltpu.VMEM),
         scratch_shapes=[
+            pltpu.SMEM((2,), jnp.int32),
             pltpu.VMEM((8,) + natural, bf),
             pltpu.VMEM((8,) + natural, bf),
             pltpu.VMEM((NY, 8, 2, 16, 2 * NF), bf),
@@ -340,14 +378,17 @@
             pltpu.VMEM((4,) + natural, bf),
             pltpu.VMEM((GROUPS, 2 * CH, 2 * CH), bf),
             pltpu.VMEM((2, NY, 2, 2, GROUPS, 2 * CH), jnp.float32),
-            dma, dma((2,)), dma((4,)), dma((6,)), dma((2,)), dma((7,)), dma((NZ,)), dma((4,)), dma((2,)), dma((2, 2)),
-            dma((3,)), dma((NY,)), dma((2, 4, 2)), dma((2, 4, 2)), dma((NZ,)), dma((NZ,)),
+            dma((2,)), dma((4,)), dma((6,)), dma((2,)), dma((7,)), dma((NZ,)), dma((4,)), dma((2,)), dma((2, 2)),
+            dma((3,)), dma((NY,)), dma((2, 4, 2)), dma((2, 4, 2)), dma((NZ,)), dma((NZ,)), dma((2,)), dma((2,)), dma((2,)),
             dma((8,)), dma((8,)), dma((8,)), dma((8,)),
         ],
         compiler_params=pltpu.CompilerParams(
             collective_id=0, has_side_effects=True, vmem_limit_bytes=28 * 1024 * 1024
         ),
-    )(plan, spectra.reshape((8,) + natural))
+    )(
+        pltpu.with_memory_space_constraint(plan, pltpu.HBM),
+        pltpu.with_memory_space_constraint(spectra.reshape((8,) + natural), pltpu.HBM),
+    )
 
 
 def lag_kernel(cross, mask_ref, table_ref, out_ref, stage, out_sems):

time: 76.3 us -> 71.5 us (0.937)
  Pallas kernels: 74.3 us -> 71.4 us
  local copies, waits for them, and re-layouts: 1.89 us -> 0.01 us
    pallas_call x1, Pallas kernels: 66.2 us -> 64.2 us  [spread(): pl.pallas_call(spread_kernel, out_shape=jax.ShapeDtypeStruct((2, NY, NZ,...]
    unnamed x8 -> x4, local copies, waits for them, and re-layouts: 1.89 us -> 0.01 us
    pallas_call x1, Pallas kernels: 8.06 us -> 7.27 us  [lags(): pl.pallas_call(lag_kernel, out_shape=jax.ShapeDtypeStruct((2, HALF, CH, L...]
where the time goes in v2:
time: 71.5 us
  Pallas kernels  71.4 us (100%)
    pallas_call x1, Pallas kernels, spread(): pl.pallas_call(spread_kernel, out_shape=jax.ShapeDtypeStruct((2, NY, NZ,...  64.2 us
    pallas_call x1, Pallas kernels, lags(): pl.pallas_call(lag_kernel, out_shape=jax.ShapeDtypeStruct((2, HALF, CH, L...  7.27 us

profile of v2, /device:TPU:1, one launch (start us, length us, event | category | flops | bytes accessed | tf_op | source)
XLA Modules:
  0.0 71.5 jit_solution(1329262707958662439)
XLA Ops:
  0.0 0.0 copy-start
  0.0 0.0 copy-start.1
  0.0 64.2 %shard_map.46 = bf16[2,4,8,512,256]{4,3,2,1,0:T(8,128)(2,1)S(1)} custom-call(s32[2]{0:T(128)} %plan_hbm.1, bf16[8,2,4,16,512]{4,3,2,1,0:T(8,128)(2,1)} %bitcast.3), custom_call_target="tpu_custom_call" | custom-call | tf_op jit(solution)/shard_map/pallas_call | solution.py:357
  64.2 0.0 copy-done
  64.2 0.0 copy-done.1
  64.2 7.3 %shard_map.47 = bf16[2,64,128,256]{3,2,1,0:T(8,128)(2,1)} custom-call(bf16[2,32,512,256]{3,2,1,0:T(8,128)(2,1)S(1)} %bitcast.2, s32[2,64,128]{2,1,0:T(8,128)S(1)} %copy-done.1, bf16[256,512]{1,0:T(8,128)(2,1)S(1)} %copy-done), custom_call_target="tpu_custom_call" | custom-call | tf_op jit(solution)/shard_map/pallas_call | solution.py:433
Async XLA Ops:
  0.0 64.2 %copy-start = (bf16[256,512]{1,0:T(8,128)(2,1)S(1)}, bf16[256,512]{1,0:T(8,128)(2,1)}, u32[]{:S(2)}) copy-start(bf16[256,512]{1,0:T(8,128)(2,1)} %constant.2.clone.table_ref) | copy-start | bytes 786436
  0.0 64.2 %copy-start.1 = (s32[2,64,128]{2,1,0:T(8,128)S(1)}, s32[2,64,128]{2,1,0:T(8,128)}, u32[]{:S(2)}) copy-start(s32[2,64,128]{2,1,0:T(8,128)} %mask_ref.1) | copy-start | bytes 196612

commit v3 on v2

--- a/solution.py
+++ b/solution.py
@@ -197,6 +197,30 @@
     def _():
         over().start()
 
+    def down(t):
+        return (z + NZ - t) % NZ
+
+    def up(t):
+        return (z + t) % NZ
+
+    def pieces(t):
+        return [(0, 0), (0, 1), (1, 2), (1, 3)] if t == 3 else [(way, d) for d in range(NY) for way in range(2)]
+
+    def piece(t, way, d):
+        return gathered.at[down(t) if way == 0 else up(t), (y + d) % NY]
+
+    def ring_piece(t, way, d):
+        ref = piece(t, way, d)
+        return remote(ref, ref, ring_send.at[way, t, d], ring_recv.at[way, t, d], at(z_=up(1) if way == 0 else down(1)))
+
+    def pass_on(slot):
+        ref = gathered.at[slot]
+        return remote(ref, ref, gc_send.at[slot], gc_recv.at[slot], at(core_=1 - core))
+
+    def pass_last(d):
+        ref = piece(4, 0, d)
+        return remote(ref, ref, last_send.at[d], last_recv.at[d], at(core_=1 - core))
+
     own = gathered.at[z, y]
 
     def over_y():
@@ -215,6 +239,8 @@
                 gathered[z, y, b, :, :, w * CH : (w + 1) * CH] = from_x[ox, w, b]
         for copy in over_y():
             copy.start()
+        for way in range(2):
+            ring_piece(0, way, 0).start()
 
     for i in range(8):
         arrived(far.at[i], hop2_recv.at[i])
@@ -258,41 +284,14 @@
         quarter = GROUPS // 4
         lax.fori_loop(quarter if part == 1 else 0, quarter if part == 0 else 2 * quarter, bins, 0, unroll=4)
 
-    def down(t):
-        return (z + NZ - t) % NZ
-
-    def up(t):
-        return (z + t) % NZ
-
-    def pieces(t):
-        return [(0, 0), (1, 1)] if t == 3 else [(0, 0), (1, 0), (0, 1), (1, 1)]
-
-    def ring_piece(t, way, half):
-        ref = gathered.at[down(t) if way == 0 else up(t), 2 * half : 2 * half + 2]
-        return remote(
-            ref, ref, ring_send.at[way, t, half], ring_recv.at[way, t, half], at(z_=up(1) if way == 0 else down(1))
-        )
-
-    def ring_arrived(t, way, half):
-        ref = gathered.at[down(t) if way == 0 else up(t), 2 * half : 2 * half + 2]
-        arrived(ref, ring_recv.at[way, t - 1, half])
-
-    def pass_on(slot):
-        ref = gathered.at[slot]
-        return remote(ref, ref, gc_send.at[slot], gc_recv.at[slot], at(core_=1 - core))
-
-    def pass_last(half):
-        ref = gathered.at[up(4), 2 * half : 2 * half + 2]
-        return remote(ref, ref, last_send.at[half], last_recv.at[half], at(core_=1 - core))
-
     def receive(t, late):
-        ways = ([(0, 0)], [(1, 1)]) if t == 4 else ([(0, 0), (1, 0)], [(0, 1), (1, 1)])
-        for way, half in ways[late]:
-            ring_arrived(t, way, half)
-            if t == 4:
-                pass_last(half).start()
-            elif (way, half) in pieces(t):
-                ring_piece(t, way, half).start()
+        for way, d in pieces(t - 1):
+            if (d >= 2) == bool(late):
+                arrived(piece(t, way, d), ring_recv.at[way, t - 1, d])
+                if t == 4:
+                    pass_last(d).start()
+                elif (way, d) in pieces(t):
+                    ring_piece(t, way, d).start()
 
     slots = [[z], [down(1), up(1)], [down(2), up(2)], [down(3), up(3)], [up(4)]]
     done = sum(slots, [])
@@ -301,10 +300,10 @@
         @pl.when(active)
         def _():
             if t == 0:
-                for v in ys:
+                for d, v in enumerate(ys):
                     arrived(gathered.at[z, v], gy_recv.at[v])
-                for way, half in pieces(0):
-                    ring_piece(0, way, half).start()
+                    for way in range(2):
+                        ring_piece(0, way, d + 1).start()
             else:
                 if t == 1:
                     receive(t, 0)
@@ -319,8 +318,8 @@
                 for slot in slots[t]:
                     arrived(gathered.at[slot], gc_recv.at[slot])
             else:
-                for half in range(2):
-                    arrived(gathered.at[up(4), 2 * half : 2 * half + 2], last_recv.at[half])
+                for d in range(NY):
+                    arrived(piece(4, 0, d), last_recv.at[d])
 
         if 0 < t < 4:
             correlate(slots[t], 0)
@@ -342,11 +341,11 @@
 
     @pl.when(active)
     def _():
-        for copy in over_y() + [pass_on(slot) for slot in done[:7]] + [pass_last(half) for half in range(2)]:
+        for copy in over_y() + [pass_on(slot) for slot in done[:7]] + [pass_last(d) for d in range(NY)]:
             copy.wait_send()
         for t in range(4):
-            for way, half in pieces(t):
-                ring_piece(t, way, half).wait_send()
+            for way, d in pieces(t):
+                ring_piece(t, way, d).wait_send()
 
 
 def spread(plan, spectra):
@@ -379,7 +378,7 @@
             pltpu.VMEM((GROUPS, 2 * CH, 2 * CH), bf),
             pltpu.VMEM((2, NY, 2, 2, GROUPS, 2 * CH), jnp.float32),
             dma((2,)), dma((4,)), dma((6,)), dma((2,)), dma((7,)), dma((NZ,)), dma((4,)), dma((2,)), dma((2, 2)),
-            dma((3,)), dma((NY,)), dma((2, 4, 2)), dma((2, 4, 2)), dma((NZ,)), dma((NZ,)), dma((2,)), dma((2,)), dma((2,)),
+            dma((3,)), dma((NY,)), dma((2, 4, NY)), dma((2, 4, NY)), dma((NZ,)), dma((NZ,)), dma((NY,)), dma((NY,)), dma((2,)),
             dma((8,)), dma((8,)), dma((8,)), dma((8,)),
         ],
         compiler_params=pltpu.CompilerParams(

time: 71.5 us -> 69.7 us (0.975)
  Pallas kernels: 71.4 us -> 69.6 us
    pallas_call x1, Pallas kernels: 64.2 us -> 62.3 us  [spread(): pl.pallas_call(spread_kernel, out_shape=jax.ShapeDtypeStruct((2, NY, NZ,...]
where the time goes in v3:
time: 69.7 us; the launch traced here: 69.6 us
  Pallas kernels  69.6 us (100%)
    pallas_call x1, Pallas kernels, spread(): pl.pallas_call(spread_kernel, out_shape=jax.ShapeDtypeStruct((2, NY, NZ,...  62.3 us
    pallas_call x1, Pallas kernels, lags(): pl.pallas_call(lag_kernel, out_shape=jax.ShapeDtypeStruct((2, HALF, CH, L...  7.28 us

profile of v3, /device:TPU:1, one launch (start us, length us, event | category | flops | bytes accessed | tf_op | source)
XLA Modules:
  0.0 69.6 jit_solution(17534324433742135788)
XLA Ops:
  0.0 0.0 copy-start
  0.0 0.0 copy-start.1
  0.0 62.3 %shard_map.46 = bf16[2,4,8,512,256]{4,3,2,1,0:T(8,128)(2,1)S(1)} custom-call(s32[2]{0:T(128)} %plan_hbm.1, bf16[8,2,4,16,512]{4,3,2,1,0:T(8,128)(2,1)} %bitcast.3), custom_call_target="tpu_custom_call" | custom-call | tf_op jit(solution)/shard_map/pallas_call | solution.py:356
  62.3 0.0 copy-done
  62.3 0.0 copy-done.1
  62.3 7.3 %shard_map.47 = bf16[2,64,128,256]{3,2,1,0:T(8,128)(2,1)} custom-call(bf16[2,32,512,256]{3,2,1,0:T(8,128)(2,1)S(1)} %bitcast.2, s32[2,64,128]{2,1,0:T(8,128)S(1)} %copy-done.1, bf16[256,512]{1,0:T(8,128)(2,1)S(1)} %copy-done), custom_call_target="tpu_custom_call" | custom-call | tf_op jit(solution)/shard_map/pallas_call | solution.py:432
Async XLA Ops:
  0.0 62.3 %copy-start = (bf16[256,512]{1,0:T(8,128)(2,1)S(1)}, bf16[256,512]{1,0:T(8,128)(2,1)}, u32[]{:S(2)}) copy-start(bf16[256,512]{1,0:T(8,128)(2,1)} %constant.2.clone.table_ref) | copy-start | bytes 786436
  0.0 62.3 %copy-start.1 = (s32[2,64,128]{2,1,0:T(8,128)S(1)}, s32[2,64,128]{2,1,0:T(8,128)}, u32[]{:S(2)}) copy-start(s32[2,64,128]{2,1,0:T(8,128)} %mask_ref.1) | copy-start | bytes 196612

commit v4 on v3

--- a/solution.py
+++ b/solution.py
@@ -39,7 +39,7 @@
 
 def spread_kernel(
     plan_hbm, spec_ref, cross,
-    plan_ref, near, far, from_y, relay_p, relay_m, to_core, from_core, to_z, from_z, relay_z, to_x, from_x,
+    plan_ref, near, far, from_y, relay_p, relay_m, to_z, from_z, relay_z, to_x, from_x,
     gathered, transit_p, transit_m, weights, sources,
     y_send, y_recv, relay_sems, core_sems, z_send, z_recv, zr_sems, x_send, x_recv,
     gy_send, gy_recv, ring_send, ring_recv, gc_send, gc_recv, last_send, last_recv, in_sems,
@@ -72,7 +72,7 @@
     ys = [(y + d) % NY for d in range(1, NY)]
     zs = [(z + d) % NZ for d in range(1, NZ)]
     peers = [at(y_=v) for v in ys] + [at(z_=v) for v in zs] + [at(core_=1 - core)]
-    peers += [plus, minus, at(win_=1 - win)]
+    peers += [plus, minus, at(win_=1 - win), at(y_=ys[0], core_=1 - core), at(y_=ys[2], core_=1 - core)]
     barrier = pltpu.get_barrier_semaphore()
     for peer in peers:
         pl.semaphore_signal(barrier, inc=1, device_id=peer, device_id_type=MESH)
@@ -87,8 +87,11 @@
     next_y, across, last_y = ys
     go(remote(spec_ref.at[0:4, :, across], relay_p, relay_sems.at[0], relay_sems.at[1], at(y_=next_y)))
     go(remote(spec_ref.at[4:8, :, across], relay_m, relay_sems.at[2], relay_sems.at[3], at(y_=last_y)))
-    go(remote(spec_ref.at[:, :, next_y], from_y.at[y], y_send.at[0], y_recv.at[0], at(y_=next_y)))
-    go(remote(spec_ref.at[:, :, last_y], from_y.at[y], y_send.at[1], y_recv.at[1], at(y_=last_y)))
+    mine = from_y.at[y, core]
+    for h in range(2):
+        go(remote(spec_ref.at[:, h, next_y], mine, y_send.at[0, h], y_recv.at[0, core], at(y_=next_y, core_=h)))
+        go(remote(spec_ref.at[:, h, last_y], mine, y_send.at[1, h], y_recv.at[1, core], at(y_=last_y, core_=h)))
+    go(remote(spec_ref.at[:, 1 - core, y], mine, core_sems.at[0], core_sems.at[1], at(core_=1 - core)))
     for i in range(4):
         go(remote(spec_ref.at[i], transit_p.at[i], hop1_send.at[i], hop1_recv.at[i], plus))
         go(remote(spec_ref.at[4 + i], transit_m.at[i], hop1_send.at[4 + i], hop1_recv.at[4 + i], minus))
@@ -113,23 +116,17 @@
 
     for load in loads:
         load.wait()
-    from_y[y] = near[:, :, y]
+    from_y[y, core] = near[:, core, y]
     arrived(relay_p, relay_sems.at[1])
-    go(remote(relay_p, from_y.at[last_y, 0:4], relay_sems.at[4], y_recv.at[2], at(y_=next_y)))
+    place = from_y.at[last_y, core, 0:4]
+    for h in range(2):
+        go(remote(relay_p.at[:, h], place, y_send.at[2, h], y_recv.at[2, core], at(y_=next_y, core_=h)))
     arrived(relay_m, relay_sems.at[3])
-    go(remote(relay_m, from_y.at[next_y, 4:8], relay_sems.at[5], y_recv.at[3], at(y_=last_y)))
+    place = from_y.at[next_y, core, 4:8]
+    for h in range(2):
+        go(remote(relay_m.at[:, h], place, y_send.at[3, h], y_recv.at[3, core], at(y_=last_y, core_=h)))
     window_pair(near, win)
 
-    arrived(from_y.at[last_y], y_recv.at[0])
-    arrived(from_y.at[next_y], y_recv.at[1])
-    arrived(from_y.at[across, 0:4], y_recv.at[2])
-    arrived(from_y.at[across, 4:8], y_recv.at[3])
-    for b in range(2):
-        oy = owner_of(plan_ref, b)[0]
-        to_core[b] = from_y[oy, :, 1 - core]
-        from_core[core, b] = from_y[oy, :, core]
-
-    go(remote(to_core, from_core.at[core], core_sems.at[0], core_sems.at[1], at(core_=1 - core)))
     def forward(i):
         arrived(transit_p.at[i], hop1_recv.at[i])
         go(remote(transit_p.at[i], far.at[i], hop2_send.at[i], hop2_recv.at[i], plus))
@@ -138,10 +135,15 @@
 
     for i in range(3):
         forward(i)
-    arrived(from_core.at[1 - core], core_sems.at[1])
+    arrived(from_y.at[y, 1 - core], core_sems.at[1])
+    for k in range(2):
+        arrived(from_y.at[last_y, k], y_recv.at[0, k])
+        arrived(from_y.at[next_y, k], y_recv.at[1, k])
+        arrived(from_y.at[across, k, 0:4], y_recv.at[2, k])
+        arrived(from_y.at[across, k, 4:8], y_recv.at[3, k])
     for b in range(2):
-        picked = from_core[owner_of(plan_ref, b)[3], b].astype(jnp.float32)
-        picked = jnp.transpose(picked, (1, 0, 2))
+        oy, _, _, oc = owner_of(plan_ref, b)
+        picked = jnp.transpose(from_y[oy, oc].astype(jnp.float32), (1, 0, 2))
         picked = jnp.concatenate([picked[:, :, :NF], picked[:, :, NF:]], 1)
         to_z[:, b] = picked.astype(jnp.bfloat16).reshape(NZ, 2, 16, NF)
 
@@ -362,11 +364,9 @@
             pltpu.SMEM((2,), jnp.int32),
             pltpu.VMEM((8,) + natural, bf),
             pltpu.VMEM((8,) + natural, bf),
-            pltpu.VMEM((NY, 8, 2, 16, 2 * NF), bf),
+            pltpu.VMEM((NY, 2, 8, 16, 2 * NF), bf),
             pltpu.VMEM((4, 2, 16, 2 * NF), bf),
             pltpu.VMEM((4, 2, 16, 2 * NF), bf),
-            pltpu.VMEM((2, 8, 16, 2 * NF), bf),
-            pltpu.VMEM((2, 2, 8, 16, 2 * NF), bf),
             pltpu.VMEM((NZ, 2) + piece, bf),
             pltpu.VMEM((NZ, 2) + piece, bf),
             pltpu.VMEM(piece, bf),
@@ -377,7 +377,7 @@
             pltpu.VMEM((4,) + natural, bf),
             pltpu.VMEM((GROUPS, 2 * CH, 2 * CH), bf),
             pltpu.VMEM((2, NY, 2, 2, GROUPS, 2 * CH), jnp.float32),
-            dma((2,)), dma((4,)), dma((6,)), dma((2,)), dma((7,)), dma((NZ,)), dma((4,)), dma((2,)), dma((2, 2)),
+            dma((4, 2)), dma((4, 2)), dma((4,)), dma((2,)), dma((7,)), dma((NZ,)), dma((4,)), dma((2,)), dma((2, 2)),
             dma((3,)), dma((NY,)), dma((2, 4, NY)), dma((2, 4, NY)), dma((NZ,)), dma((NZ,)), dma((NY,)), dma((NY,)), dma((2,)),
             dma((8,)), dma((8,)), dma((8,)), dma((8,)),
         ],

time: 69.7 us -> 69.4 us (level)
  no operation moved by 1% of the time
where the time goes in v4:
time: 69.4 us
  Pallas kernels  69.3 us (100%)
    pallas_call x1, Pallas kernels, spread(): pl.pallas_call(spread_kernel, out_shape=jax.ShapeDtypeStruct((2, NY, NZ,...  62 us
    pallas_call x1, Pallas kernels, lags(): pl.pallas_call(lag_kernel, out_shape=jax.ShapeDtypeStruct((2, HALF, CH, L...  7.28 us

profile of v4, /device:TPU:1, one launch (start us, length us, event | category | flops | bytes accessed | tf_op | source)
XLA Modules:
  0.0 69.4 jit_solution(9453977395970017033)
XLA Ops:
  0.0 0.0 copy-start
  0.0 0.0 copy-start.1
  0.0 62.0 %shard_map.46 = bf16[2,4,8,512,256]{4,3,2,1,0:T(8,128)(2,1)S(1)} custom-call(s32[2]{0:T(128)} %plan_hbm.1, bf16[8,2,4,16,512]{4,3,2,1,0:T(8,128)(2,1)} %bitcast.3), custom_call_target="tpu_custom_call" | custom-call | tf_op jit(solution)/shard_map/pallas_call | solution.py:358
  62.1 0.0 copy-done
  62.1 0.0 copy-done.1
  62.1 7.3 %shard_map.47 = bf16[2,64,128,256]{3,2,1,0:T(8,128)(2,1)} custom-call(bf16[2,32,512,256]{3,2,1,0:T(8,128)(2,1)S(1)} %bitcast.2, s32[2,64,128]{2,1,0:T(8,128)S(1)} %copy-done.1, bf16[256,512]{1,0:T(8,128)(2,1)S(1)} %copy-done), custom_call_target="tpu_custom_call" | custom-call | tf_op jit(solution)/shard_map/pallas_call | solution.py:432
Async XLA Ops:
  0.0 62.1 %copy-start = (bf16[256,512]{1,0:T(8,128)(2,1)S(1)}, bf16[256,512]{1,0:T(8,128)(2,1)}, u32[]{:S(2)}) copy-start(bf16[256,512]{1,0:T(8,128)(2,1)} %constant.2.clone.table_ref) | copy-start | bytes 786436
  0.0 62.1 %copy-start.1 = (s32[2,64,128]{2,1,0:T(8,128)S(1)}, s32[2,64,128]{2,1,0:T(8,128)}, u32[]{:S(2)}) copy-start(s32[2,64,128]{2,1,0:T(8,128)} %mask_ref.1) | copy-start | bytes 196612

commit v5 on v4

--- a/solution.py
+++ b/solution.py
@@ -39,12 +39,13 @@
 
 def spread_kernel(
     plan_hbm, spec_ref, cross,
-    plan_ref, near, far, from_y, relay_p, relay_m, to_z, from_z, relay_z, to_x, from_x,
+    plan_ref, near, far, from_y_real, from_y_imag, relay_p, relay_m, to_z, from_z, relay_z, to_x, from_x,
     gathered, transit_p, transit_m, weights, sources,
     y_send, y_recv, relay_sems, core_sems, z_send, z_recv, zr_sems, x_send, x_recv,
     gy_send, gy_recv, ring_send, ring_recv, gc_send, gc_recv, last_send, last_recv, in_sems,
     hop1_send, hop1_recv, hop2_send, hop2_recv,
 ):
+    from_y = (from_y_real, from_y_imag)
     rx, win = lax.axis_index("rx"), lax.axis_index("win")
     core, z, x_lo, y = rx % 2, (rx // 2) % NZ, (rx // 16) % 2, rx // 32
 
@@ -85,13 +86,45 @@
         sent.append(copy)
 
     next_y, across, last_y = ys
-    go(remote(spec_ref.at[0:4, :, across], relay_p, relay_sems.at[0], relay_sems.at[1], at(y_=next_y)))
-    go(remote(spec_ref.at[4:8, :, across], relay_m, relay_sems.at[2], relay_sems.at[3], at(y_=last_y)))
-    mine = from_y.at[y, core]
-    for h in range(2):
-        go(remote(spec_ref.at[:, h, next_y], mine, y_send.at[0, h], y_recv.at[0, core], at(y_=next_y, core_=h)))
-        go(remote(spec_ref.at[:, h, last_y], mine, y_send.at[1, h], y_recv.at[1, core], at(y_=last_y, core_=h)))
-    go(remote(spec_ref.at[:, 1 - core, y], mine, core_sems.at[0], core_sems.at[1], at(core_=1 - core)))
+
+    def scatter_y(c):
+        part = pl.ds(c * NF, NF)
+        rs, ss, rr = relay_sems.at[c], y_send.at[c], y_recv.at[c]
+        go(remote(spec_ref.at[0:4, :, across, :, part], relay_p.at[c], rs.at[0], rs.at[1], at(y_=next_y)))
+        go(remote(spec_ref.at[4:8, :, across, :, part], relay_m.at[c], rs.at[2], rs.at[3], at(y_=last_y)))
+        mine = from_y[c].at[y, core]
+        for h in range(2):
+            there = at(y_=next_y, core_=h)
+            go(remote(spec_ref.at[:, h, next_y, :, part], mine, ss.at[0, h], rr.at[0, core], there))
+            there = at(y_=last_y, core_=h)
+            go(remote(spec_ref.at[:, h, last_y, :, part], mine, ss.at[1, h], rr.at[1, core], there))
+        sibling = at(core_=1 - core)
+        go(remote(spec_ref.at[:, 1 - core, y, :, part], mine, core_sems.at[c, 0], core_sems.at[c, 1], sibling))
+
+    def relay_y(c):
+        rs, ss, rr = relay_sems.at[c], y_send.at[c], y_recv.at[c]
+        arrived(relay_p.at[c], rs.at[1])
+        place = from_y[c].at[last_y, core, 0:4]
+        for h in range(2):
+            go(remote(relay_p.at[c, :, h], place, ss.at[2, h], rr.at[2, core], at(y_=next_y, core_=h)))
+        arrived(relay_m.at[c], rs.at[3])
+        place = from_y[c].at[next_y, core, 4:8]
+        for h in range(2):
+            go(remote(relay_m.at[c, :, h], place, ss.at[3, h], rr.at[3, core], at(y_=last_y, core_=h)))
+
+    def gathered_y(c):
+        arrived(from_y[c].at[y, 1 - core], core_sems.at[c, 1])
+        for k in range(2):
+            arrived(from_y[c].at[last_y, k], y_recv.at[c, 0, k])
+            arrived(from_y[c].at[next_y, k], y_recv.at[c, 1, k])
+            arrived(from_y[c].at[across, k, 0:4], y_recv.at[c, 2, k])
+            arrived(from_y[c].at[across, k, 4:8], y_recv.at[c, 3, k])
+        for b in range(2):
+            oy, _, _, oc = owner_of(plan_ref, b)
+            picked = jnp.transpose(from_y[c][oy, oc].astype(jnp.float32), (1, 0, 2))
+            to_z[c, :, b] = picked.reshape(NZ, 16, NF).astype(jnp.bfloat16)
+
+    scatter_y(0)
     for i in range(4):
         go(remote(spec_ref.at[i], transit_p.at[i], hop1_send.at[i], hop1_recv.at[i], plus))
         go(remote(spec_ref.at[4 + i], transit_m.at[i], hop1_send.at[4 + i], hop1_recv.at[4 + i], minus))
@@ -116,45 +149,38 @@
 
     for load in loads:
         load.wait()
-    from_y[y, core] = near[:, core, y]
-    arrived(relay_p, relay_sems.at[1])
-    place = from_y.at[last_y, core, 0:4]
-    for h in range(2):
-        go(remote(relay_p.at[:, h], place, y_send.at[2, h], y_recv.at[2, core], at(y_=next_y, core_=h)))
-    arrived(relay_m, relay_sems.at[3])
-    place = from_y.at[next_y, core, 4:8]
-    for h in range(2):
-        go(remote(relay_m.at[:, h], place, y_send.at[3, h], y_recv.at[3, core], at(y_=last_y, core_=h)))
+    for c in range(2):
+        from_y[c][y, core] = near[:, core, y, :, c * NF : (c + 1) * NF]
+    relay_y(0)
+    scatter_y(1)
     window_pair(near, win)
-
-    def forward(i):
+    relay_y(1)
+
+    opposite, three_down, one_down = zs[3], zs[4], zs[6]
+
+    def scatter_z(c):
+        gathered_y(c)
+        rs, ss, rr = zr_sems.at[c], z_send.at[c], z_recv.at[c]
+        go(remote(to_z.at[c, opposite, 1], relay_z.at[c], rs.at[0], rs.at[1], at(z_=three_down)))
+        go(remote(to_z.at[c, opposite, 0], from_z.at[c, z, 0], ss.at[3], rr.at[z], at(z_=opposite)))
+        for d, v in enumerate(zs):
+            if d != 3:
+                go(remote(to_z.at[c, v], from_z.at[c, z], ss.at[d], rr.at[z], at(z_=v)))
+        from_z[c, z] = to_z[c, z]
+
+    def relay_back(c):
+        arrived(relay_z.at[c], zr_sems.at[c, 1])
+        go(remote(relay_z.at[c], from_z.at[c, zs[2], 1], zr_sems.at[c, 2], zr_sems.at[c, 3], at(z_=one_down)))
+
+    scatter_z(0)
+    relay_back(0)
+    scatter_z(1)
+    for i in range(4):
         arrived(transit_p.at[i], hop1_recv.at[i])
         go(remote(transit_p.at[i], far.at[i], hop2_send.at[i], hop2_recv.at[i], plus))
         arrived(transit_m.at[i], hop1_recv.at[4 + i])
         go(remote(transit_m.at[i], far.at[4 + i], hop2_send.at[4 + i], hop2_recv.at[4 + i], minus))
-
-    for i in range(3):
-        forward(i)
-    arrived(from_y.at[y, 1 - core], core_sems.at[1])
-    for k in range(2):
-        arrived(from_y.at[last_y, k], y_recv.at[0, k])
-        arrived(from_y.at[next_y, k], y_recv.at[1, k])
-        arrived(from_y.at[across, k, 0:4], y_recv.at[2, k])
-        arrived(from_y.at[across, k, 4:8], y_recv.at[3, k])
-    for b in range(2):
-        oy, _, _, oc = owner_of(plan_ref, b)
-        picked = jnp.transpose(from_y[oy, oc].astype(jnp.float32), (1, 0, 2))
-        picked = jnp.concatenate([picked[:, :, :NF], picked[:, :, NF:]], 1)
-        to_z[:, b] = picked.astype(jnp.bfloat16).reshape(NZ, 2, 16, NF)
-
-    opposite, three_down, one_down = zs[3], zs[4], zs[6]
-    go(remote(to_z.at[opposite, :, 1], relay_z, zr_sems.at[0], zr_sems.at[1], at(z_=three_down)))
-    go(remote(to_z.at[opposite, :, 0], from_z.at[z, :, 0], z_send.at[3], z_recv.at[z], at(z_=opposite)))
-    for d, v in enumerate(zs):
-        if d != 3:
-            go(remote(to_z.at[v], from_z.at[z], z_send.at[d], z_recv.at[z], at(z_=v)))
-    from_z[z] = to_z[z]
-    forward(3)
+    relay_back(1)
 
     shape = (GROUPS * 16, NF)
     pick_group = (lax.broadcasted_iota(jnp.int32, shape, 1) >> 3) == (lax.broadcasted_iota(jnp.int32, shape, 0) >> 4)
@@ -167,26 +193,27 @@
     in_row = lax.broadcasted_iota(jnp.int32, (GROUPS, GROUPS * 16), 1)
     same_group = ((in_row >> 4) == out_row).astype(jnp.float32).astype(jnp.bfloat16)
 
-    arrived(relay_z, zr_sems.at[1])
-    go(remote(relay_z, from_z.at[zs[2], :, 1], zr_sems.at[2], zr_sems.at[3], at(z_=one_down)))
-    for d, v in enumerate(zs):
-        if d != 3:
-            arrived(from_z.at[v], z_recv.at[v])
-    arrived(from_z.at[opposite, :, 0], z_recv.at[opposite])
-    arrived(from_z.at[opposite, :, 1], zr_sems.at[3])
-
-    def regroup(i, carry):
-        b, e = i // 2, i % 2
-        rows = from_z[owner_of(plan_ref, b)[2], b, e].astype(jnp.float32).reshape(1, 16, NF)
-        rows = jnp.broadcast_to(rows, (GROUPS, 16, NF)).reshape(GROUPS * 16, NF)
-        rows = jnp.where(pick_group, rows, 0.0).astype(jnp.bfloat16)
-        moved = jnp.dot(rows, same_place, preferred_element_type=jnp.float32)
-        moved = jnp.where(pick_row, moved, 0.0).astype(jnp.bfloat16)
-        done = jnp.dot(same_group, moved, preferred_element_type=jnp.float32)
-        to_x[b, e] = done.astype(jnp.bfloat16)
+    for c in range(2):
+        for d, v in enumerate(zs):
+            if d != 3:
+                arrived(from_z.at[c, v], z_recv.at[c, v])
+        arrived(from_z.at[c, opposite, 0], z_recv.at[c, opposite])
+        arrived(from_z.at[c, opposite, 1], zr_sems.at[c, 3])
+
+    def regroup(b, carry):
+        oz = owner_of(plan_ref, b)[2]
+        parts = [from_z[c, oz, b].astype(jnp.float32) for c in range(2)]
+        for e in range(2):
+            rows = jnp.concatenate([part[8 * e : 8 * e + 8] for part in parts], 0).reshape(1, 16, NF)
+            rows = jnp.broadcast_to(rows, (GROUPS, 16, NF)).reshape(GROUPS * 16, NF)
+            rows = jnp.where(pick_group, rows, 0.0).astype(jnp.bfloat16)
+            moved = jnp.dot(rows, same_place, preferred_element_type=jnp.float32)
+            moved = jnp.where(pick_row, moved, 0.0).astype(jnp.bfloat16)
+            done = jnp.dot(same_group, moved, preferred_element_type=jnp.float32)
+            to_x[b, e] = done.astype(jnp.bfloat16)
         return carry
 
-    lax.fori_loop(0, 4, regroup, 0, unroll=2)
+    lax.fori_loop(0, 2, regroup, 0, unroll=2)
 
     active = win == core
     there = from_x.at[x_lo, win]
@@ -352,7 +379,6 @@
 
 def spread(plan, spectra):
     bf = jnp.bfloat16
-    piece = (2, 16, NF)
     dma = pltpu.SemaphoreType.DMA
     natural = (2, NY, 16, 2 * NF)
     return pl.pallas_call(
@@ -364,12 +390,13 @@
             pltpu.SMEM((2,), jnp.int32),
             pltpu.VMEM((8,) + natural, bf),
             pltpu.VMEM((8,) + natural, bf),
-            pltpu.VMEM((NY, 2, 8, 16, 2 * NF), bf),
-            pltpu.VMEM((4, 2, 16, 2 * NF), bf),
-            pltpu.VMEM((4, 2, 16, 2 * NF), bf),
-            pltpu.VMEM((NZ, 2) + piece, bf),
-            pltpu.VMEM((NZ, 2) + piece, bf),
-            pltpu.VMEM(piece, bf),
+            pltpu.VMEM((NY, 2, 8, 16, NF), bf),
+            pltpu.VMEM((NY, 2, 8, 16, NF), bf),
+            pltpu.VMEM((2, 4, 2, 16, NF), bf),
+            pltpu.VMEM((2, 4, 2, 16, NF), bf),
+            pltpu.VMEM((2, NZ, 2, 16, NF), bf),
+            pltpu.VMEM((2, NZ, 2, 16, NF), bf),
+            pltpu.VMEM((2, 16, NF), bf),
             pltpu.VMEM((2, 2, GROUPS, CH), bf),
             pltpu.VMEM((2, 2, 2, 2, GROUPS, CH), bf),
             pltpu.VMEM((NZ, NY, 2, 2, GROUPS, 2 * CH), bf),
@@ -377,7 +404,8 @@
             pltpu.VMEM((4,) + natural, bf),
             pltpu.VMEM((GROUPS, 2 * CH, 2 * CH), bf),
             pltpu.VMEM((2, NY, 2, 2, GROUPS, 2 * CH), jnp.float32),
-            dma((4, 2)), dma((4, 2)), dma((4,)), dma((2,)), dma((7,)), dma((NZ,)), dma((4,)), dma((2,)), dma((2, 2)),
+            dma((2, 4, 2)), dma((2, 4, 2)), dma((2, 4)), dma((2, 2)), dma((2, 7)), dma((2, NZ)), dma((2, 4)),
+            dma((2,)), dma((2, 2)),
             dma((3,)), dma((NY,)), dma((2, 4, NY)), dma((2, 4, NY)), dma((NZ,)), dma((NZ,)), dma((NY,)), dma((NY,)), dma((2,)),
             dma((8,)), dma((8,)), dma((8,)), dma((8,)),
         ],

time: 69.4 us -> 70.9 us (1.022)
  Pallas kernels: 69.3 us -> 70.8 us
    pallas_call x1, Pallas kernels: 62 us -> 63.5 us  [spread(): pl.pallas_call(spread_kernel, out_shape=jax.ShapeDtypeStruct((2, NY, NZ,...]
where the time goes in v5:
time: 70.9 us; the launch traced here: 70.8 us
  Pallas kernels  70.8 us (100%)
    pallas_call x1, Pallas kernels, spread(): pl.pallas_call(spread_kernel, out_shape=jax.ShapeDtypeStruct((2, NY, NZ,...  63.5 us
    pallas_call x1, Pallas kernels, lags(): pl.pallas_call(lag_kernel, out_shape=jax.ShapeDtypeStruct((2, HALF, CH, L...  7.28 us

profile of v5, /device:TPU:1, one launch (start us, length us, event | category | flops | bytes accessed | tf_op | source)
XLA Modules:
  0.0 70.8 jit_solution(1674356671453580806)
XLA Ops:
  0.0 0.0 copy-start
  0.0 0.0 copy-start.1
  0.0 63.5 %shard_map.46 = bf16[2,4,8,512,256]{4,3,2,1,0:T(8,128)(2,1)S(1)} custom-call(s32[2]{0:T(128)} %plan_hbm.1, bf16[8,2,4,16,512]{4,3,2,1,0:T(8,128)(2,1)} %bitcast.3), custom_call_target="tpu_custom_call" | custom-call | tf_op jit(solution)/shard_map/pallas_call | solution.py:384
  63.5 0.0 copy-done
  63.5 0.0 copy-done.1
  63.5 7.3 %shard_map.47 = bf16[2,64,128,256]{3,2,1,0:T(8,128)(2,1)} custom-call(bf16[2,32,512,256]{3,2,1,0:T(8,128)(2,1)S(1)} %bitcast.2, s32[2,64,128]{2,1,0:T(8,128)S(1)} %copy-done.1, bf16[256,512]{1,0:T(8,128)(2,1)S(1)} %copy-done), custom_call_target="tpu_custom_call" | custom-call | tf_op jit(solution)/shard_map/pallas_call | solution.py:460
Async XLA Ops:
  0.0 63.5 %copy-start = (bf16[256,512]{1,0:T(8,128)(2,1)S(1)}, bf16[256,512]{1,0:T(8,128)(2,1)}, u32[]{:S(2)}) copy-start(bf16[256,512]{1,0:T(8,128)(2,1)} %constant.2.clone.table_ref) | copy-start | bytes 786436
  0.0 63.5 %copy-start.1 = (s32[2,64,128]{2,1,0:T(8,128)S(1)}, s32[2,64,128]{2,1,0:T(8,128)}, u32[]{:S(2)}) copy-start(s32[2,64,128]{2,1,0:T(8,128)} %mask_ref.1) | copy-start | bytes 196612

commit v6 on v4

--- a/solution.py
+++ b/solution.py
@@ -85,18 +85,23 @@
         sent.append(copy)
 
     next_y, across, last_y = ys
+
+    def hop1(i):
+        go(remote(spec_ref.at[i], transit_p.at[i], hop1_send.at[i], hop1_recv.at[i], plus))
+        go(remote(spec_ref.at[4 + i], transit_m.at[i], hop1_send.at[4 + i], hop1_recv.at[4 + i], minus))
+
     go(remote(spec_ref.at[0:4, :, across], relay_p, relay_sems.at[0], relay_sems.at[1], at(y_=next_y)))
     go(remote(spec_ref.at[4:8, :, across], relay_m, relay_sems.at[2], relay_sems.at[3], at(y_=last_y)))
+    hop1(0)
     mine = from_y.at[y, core]
     for h in range(2):
         go(remote(spec_ref.at[:, h, next_y], mine, y_send.at[0, h], y_recv.at[0, core], at(y_=next_y, core_=h)))
         go(remote(spec_ref.at[:, h, last_y], mine, y_send.at[1, h], y_recv.at[1, core], at(y_=last_y, core_=h)))
     go(remote(spec_ref.at[:, 1 - core, y], mine, core_sems.at[0], core_sems.at[1], at(core_=1 - core)))
-    for i in range(4):
-        go(remote(spec_ref.at[i], transit_p.at[i], hop1_send.at[i], hop1_recv.at[i], plus))
-        go(remote(spec_ref.at[4 + i], transit_m.at[i], hop1_send.at[4 + i], hop1_recv.at[4 + i], minus))
-
-    def window_pair(ref, side):
+    for i in range(1, 4):
+        hop1(i)
+
+    def window_pair(ref, side, first):
         def body(i, carry):
             both = [
                 ref[2 * i + k].reshape(CH, 2 * NF).astype(jnp.float32).T.reshape(2, GROUPS, 8, CH) for k in range(2)
@@ -112,11 +117,17 @@
             weights[:, pl.ds(HALF + row, 16), CH:] = a
             return carry
 
-        lax.fori_loop(0, 4, body, 0)
+        lax.fori_loop(0, 2, lambda i, carry: body(first + 2 * i, carry), 0, unroll=2)
 
     for load in loads:
         load.wait()
     from_y[y, core] = near[:, core, y]
+    def forward(i):
+        arrived(transit_p.at[i], hop1_recv.at[i])
+        go(remote(transit_p.at[i], far.at[i], hop2_send.at[i], hop2_recv.at[i], plus))
+        arrived(transit_m.at[i], hop1_recv.at[4 + i])
+        go(remote(transit_m.at[i], far.at[4 + i], hop2_send.at[4 + i], hop2_recv.at[4 + i], minus))
+
     arrived(relay_p, relay_sems.at[1])
     place = from_y.at[last_y, core, 0:4]
     for h in range(2):
@@ -125,16 +136,13 @@
     place = from_y.at[next_y, core, 4:8]
     for h in range(2):
         go(remote(relay_m.at[:, h], place, y_send.at[3, h], y_recv.at[3, core], at(y_=last_y, core_=h)))
-    window_pair(near, win)
-
-    def forward(i):
-        arrived(transit_p.at[i], hop1_recv.at[i])
-        go(remote(transit_p.at[i], far.at[i], hop2_send.at[i], hop2_recv.at[i], plus))
-        arrived(transit_m.at[i], hop1_recv.at[4 + i])
-        go(remote(transit_m.at[i], far.at[4 + i], hop2_send.at[4 + i], hop2_recv.at[4 + i], minus))
-
-    for i in range(3):
-        forward(i)
+    forward(0)
+    window_pair(near, win, 0)
+    forward(1)
+    window_pair(near, win, 1)
+
+    forward(2)
+    forward(3)
     arrived(from_y.at[y, 1 - core], core_sems.at[1])
     for k in range(2):
         arrived(from_y.at[last_y, k], y_recv.at[0, k])
@@ -154,7 +162,6 @@
         if d != 3:
             go(remote(to_z.at[v], from_z.at[z], z_send.at[d], z_recv.at[z], at(z_=v)))
     from_z[z] = to_z[z]
-    forward(3)
 
     shape = (GROUPS * 16, NF)
     pick_group = (lax.broadcasted_iota(jnp.int32, shape, 1) >> 3) == (lax.broadcasted_iota(jnp.int32, shape, 0) >> 4)
@@ -244,9 +251,11 @@
         for way in range(2):
             ring_piece(0, way, 0).start()
 
-    for i in range(8):
-        arrived(far.at[i], hop2_recv.at[i])
-    window_pair(far, 1 - win)
+    for first in range(2):
+        for i in (2 * first, 2 * first + 1):
+            arrived(far.at[i], hop2_recv.at[i])
+            arrived(far.at[4 + i], hop2_recv.at[4 + i])
+        window_pair(far, 1 - win, first)
 
     lane = lax.broadcasted_iota(jnp.int32, (1, 8, 2 * CH), 2)
     sub = lax.broadcasted_iota(jnp.int32, (1, 8, 2 * CH), 1)

time: 69.4 us -> 69.9 us (level)
  no operation moved by 1% of the time
where the time goes in v6:
time: 69.9 us; the launch traced here: 69.8 us
  Pallas kernels  69.7 us (100%)
    pallas_call x1, Pallas kernels, spread(): pl.pallas_call(spread_kernel, out_shape=jax.ShapeDtypeStruct((2, NY, NZ,...  62.5 us
    pallas_call x1, Pallas kernels, lags(): pl.pallas_call(lag_kernel, out_shape=jax.ShapeDtypeStruct((2, HALF, CH, L...  7.27 us

profile of v6, /device:TPU:1, one launch (start us, length us, event | category | flops | bytes accessed | tf_op | source)
XLA Modules:
  0.0 69.8 jit_solution(9095908405806281295)
XLA Ops:
  0.0 0.0 copy-start
  0.0 0.0 copy-start.1
  0.0 62.5 %shard_map.46 = bf16[2,4,8,512,256]{4,3,2,1,0:T(8,128)(2,1)S(1)} custom-call(s32[2]{0:T(128)} %plan_hbm.1, bf16[8,2,4,16,512]{4,3,2,1,0:T(8,128)(2,1)} %bitcast.3), custom_call_target="tpu_custom_call" | custom-call | tf_op jit(solution)/shard_map/pallas_call | solution.py:367
  62.5 0.0 copy-done
  62.5 0.0 copy-done.1
  62.5 7.3 %shard_map.47 = bf16[2,64,128,256]{3,2,1,0:T(8,128)(2,1)} custom-call(bf16[2,32,512,256]{3,2,1,0:T(8,128)(2,1)S(1)} %bitcast.2, s32[2,64,128]{2,1,0:T(8,128)S(1)} %copy-done.1, bf16[256,512]{1,0:T(8,128)(2,1)S(1)} %copy-done), custom_call_target="tpu_custom_call" | custom-call | tf_op jit(solution)/shard_map/pallas_call | solution.py:441
Async XLA Ops:
  0.0 62.5 %copy-start = (bf16[256,512]{1,0:T(8,128)(2,1)S(1)}, bf16[256,512]{1,0:T(8,128)(2,1)}, u32[]{:S(2)}) copy-start(bf16[256,512]{1,0:T(8,128)(2,1)} %constant.2.clone.table_ref) | copy-start | bytes 786436
  0.0 62.5 %copy-start.1 = (s32[2,64,128]{2,1,0:T(8,128)S(1)}, s32[2,64,128]{2,1,0:T(8,128)}, u32[]{:S(2)}) copy-start(s32[2,64,128]{2,1,0:T(8,128)} %mask_ref.1) | copy-start | bytes 196612

commit v7 on v6

--- a/solution.py
+++ b/solution.py
@@ -42,7 +42,7 @@
     plan_ref, near, far, from_y, relay_p, relay_m, to_z, from_z, relay_z, to_x, from_x,
     gathered, transit_p, transit_m, weights, sources,
     y_send, y_recv, relay_sems, core_sems, z_send, z_recv, zr_sems, x_send, x_recv,
-    gy_send, gy_recv, ring_send, ring_recv, gc_send, gc_recv, last_send, last_recv, in_sems,
+    gy_send, gy_recv, ring_send, ring_recv, gc_send, gc_recv, in_sems,
     hop1_send, hop1_recv, hop2_send, hop2_recv,
 ):
     rx, win = lax.axis_index("rx"), lax.axis_index("win")
@@ -222,13 +222,13 @@
         ref = piece(t, way, d)
         return remote(ref, ref, ring_send.at[way, t, d], ring_recv.at[way, t, d], at(z_=up(1) if way == 0 else down(1)))
 
-    def pass_on(slot):
-        ref = gathered.at[slot]
-        return remote(ref, ref, gc_send.at[slot], gc_recv.at[slot], at(core_=1 - core))
-
-    def pass_last(d):
-        ref = piece(4, 0, d)
-        return remote(ref, ref, last_send.at[d], last_recv.at[d], at(core_=1 - core))
+    def pass_on(t, way, d):
+        ref = piece(t, way, d)
+        slot = down(t) if way == 0 else up(t)
+        return remote(ref, ref, gc_send.at[slot, d], gc_recv.at[slot, d], at(core_=1 - core))
+
+    def passed(t):
+        return [(0, d) for d in range(NY)] if t in (0, 4) else [(way, d) for d in range(NY) for way in range(2)]
 
     own = gathered.at[z, y]
 
@@ -250,6 +250,7 @@
             copy.start()
         for way in range(2):
             ring_piece(0, way, 0).start()
+        pass_on(0, 0, 0).start()
 
     for first in range(2):
         for i in (2 * first, 2 * first + 1):
@@ -293,19 +294,17 @@
             return carry
 
         quarter = GROUPS // 4
-        lax.fori_loop(quarter if part == 1 else 0, quarter if part == 0 else 2 * quarter, bins, 0, unroll=4)
+        lax.fori_loop(quarter if part == 1 else 0, quarter if part == 0 else 2 * quarter, bins, 0, unroll=8)
 
     def receive(t, late):
         for way, d in pieces(t - 1):
             if (d >= 2) == bool(late):
                 arrived(piece(t, way, d), ring_recv.at[way, t - 1, d])
-                if t == 4:
-                    pass_last(d).start()
-                elif (way, d) in pieces(t):
+                if t < 4 and (way, d) in pieces(t):
                     ring_piece(t, way, d).start()
+                pass_on(t, way, d).start()
 
     slots = [[z], [down(1), up(1)], [down(2), up(2)], [down(3), up(3)], [up(4)]]
-    done = sum(slots, [])
     for t in range(5):
 
         @pl.when(active)
@@ -315,22 +314,17 @@
                     arrived(gathered.at[z, v], gy_recv.at[v])
                     for way in range(2):
                         ring_piece(0, way, d + 1).start()
+                    pass_on(0, 0, d + 1).start()
             else:
                 if t == 1:
                     receive(t, 0)
                 receive(t, 1)
-            if t < 4:
-                for slot in slots[t]:
-                    pass_on(slot).start()
 
         @pl.when(win != core)
         def _():
-            if t < 4:
-                for slot in slots[t]:
-                    arrived(gathered.at[slot], gc_recv.at[slot])
-            else:
-                for d in range(NY):
-                    arrived(piece(4, 0, d), last_recv.at[d])
+            for way, d in passed(t):
+                slot = down(t) if way == 0 else up(t)
+                arrived(piece(t, way, d), gc_recv.at[slot, d])
 
         if 0 < t < 4:
             correlate(slots[t], 0)
@@ -352,7 +346,7 @@
 
     @pl.when(active)
     def _():
-        for copy in over_y() + [pass_on(slot) for slot in done[:7]] + [pass_last(d) for d in range(NY)]:
+        for copy in over_y() + [pass_on(t, way, d) for t in range(5) for way, d in passed(t)]:
             copy.wait_send()
         for t in range(4):
             for way, d in pieces(t):
@@ -387,7 +381,7 @@
             pltpu.VMEM((GROUPS, 2 * CH, 2 * CH), bf),
             pltpu.VMEM((2, NY, 2, 2, GROUPS, 2 * CH), jnp.float32),
             dma((4, 2)), dma((4, 2)), dma((4,)), dma((2,)), dma((7,)), dma((NZ,)), dma((4,)), dma((2,)), dma((2, 2)),
-            dma((3,)), dma((NY,)), dma((2, 4, NY)), dma((2, 4, NY)), dma((NZ,)), dma((NZ,)), dma((NY,)), dma((NY,)), dma((2,)),
+            dma((3,)), dma((NY,)), dma((2, 4, NY)), dma((2, 4, NY)), dma((NZ, NY)), dma((NZ, NY)), dma((2,)),
             dma((8,)), dma((8,)), dma((8,)), dma((8,)),
         ],
         compiler_params=pltpu.CompilerParams(

time: 69.9 us -> 69.6 us (level)
  no operation moved by 1% of the time
where the time goes in v7:
time: 69.6 us; the launch traced here: 69.5 us
  Pallas kernels  69.5 us (100%)
    pallas_call x1, Pallas kernels, spread(): pl.pallas_call(spread_kernel, out_shape=jax.ShapeDtypeStruct((2, NY, NZ,...  62.2 us
    pallas_call x1, Pallas kernels, lags(): pl.pallas_call(lag_kernel, out_shape=jax.ShapeDtypeStruct((2, HALF, CH, L...  7.27 us

profile of v7, /device:TPU:1, one launch (start us, length us, event | category | flops | bytes accessed | tf_op | source)
XLA Modules:
  0.0 69.5 jit_solution(10659784502310308716)
XLA Ops:
  0.0 0.0 copy-start
  0.0 0.0 copy-start.1
  0.0 62.2 %shard_map.46 = bf16[2,4,8,512,256]{4,3,2,1,0:T(8,128)(2,1)S(1)} custom-call(s32[2]{0:T(128)} %plan_hbm.1, bf16[8,2,4,16,512]{4,3,2,1,0:T(8,128)(2,1)} %bitcast.3), custom_call_target="tpu_custom_call" | custom-call | tf_op jit(solution)/shard_map/pallas_call | solution.py:361
  62.2 0.0 copy-done
  62.2 0.0 copy-done.1
  62.2 7.3 %shard_map.47 = bf16[2,64,128,256]{3,2,1,0:T(8,128)(2,1)} custom-call(bf16[2,32,512,256]{3,2,1,0:T(8,128)(2,1)S(1)} %bitcast.2, s32[2,64,128]{2,1,0:T(8,128)S(1)} %copy-done.1, bf16[256,512]{1,0:T(8,128)(2,1)S(1)} %copy-done), custom_call_target="tpu_custom_call" | custom-call | tf_op jit(solution)/shard_map/pallas_call | solution.py:435
Async XLA Ops:
  0.0 62.2 %copy-start = (bf16[256,512]{1,0:T(8,128)(2,1)S(1)}, bf16[256,512]{1,0:T(8,128)(2,1)}, u32[]{:S(2)}) copy-start(bf16[256,512]{1,0:T(8,128)(2,1)} %constant.2.clone.table_ref) | copy-start | bytes 786436
  0.0 62.2 %copy-start.1 = (s32[2,64,128]{2,1,0:T(8,128)S(1)}, s32[2,64,128]{2,1,0:T(8,128)}, u32[]{:S(2)}) copy-start(s32[2,64,128]{2,1,0:T(8,128)} %mask_ref.1) | copy-start | bytes 196612

commit v8 on v7

--- a/solution.py
+++ b/solution.py
@@ -98,8 +98,7 @@
         go(remote(spec_ref.at[:, h, next_y], mine, y_send.at[0, h], y_recv.at[0, core], at(y_=next_y, core_=h)))
         go(remote(spec_ref.at[:, h, last_y], mine, y_send.at[1, h], y_recv.at[1, core], at(y_=last_y, core_=h)))
     go(remote(spec_ref.at[:, 1 - core, y], mine, core_sems.at[0], core_sems.at[1], at(core_=1 - core)))
-    for i in range(1, 4):
-        hop1(i)
+    hop1(1)
 
     def window_pair(ref, side, first):
         def body(i, carry):
@@ -136,13 +135,13 @@
     place = from_y.at[next_y, core, 4:8]
     for h in range(2):
         go(remote(relay_m.at[:, h], place, y_send.at[3, h], y_recv.at[3, core], at(y_=last_y, core_=h)))
+    hop1(2)
+    window_pair(near, win, 0)
+    hop1(3)
+    window_pair(near, win, 1)
     forward(0)
-    window_pair(near, win, 0)
     forward(1)
-    window_pair(near, win, 1)
-
     forward(2)
-    forward(3)
     arrived(from_y.at[y, 1 - core], core_sems.at[1])
     for k in range(2):
         arrived(from_y.at[last_y, k], y_recv.at[0, k])
@@ -162,6 +161,7 @@
         if d != 3:
             go(remote(to_z.at[v], from_z.at[z], z_send.at[d], z_recv.at[z], at(z_=v)))
     from_z[z] = to_z[z]
+    forward(3)
 
     shape = (GROUPS * 16, NF)
     pick_group = (lax.broadcasted_iota(jnp.int32, shape, 1) >> 3) == (lax.broadcasted_iota(jnp.int32, shape, 0) >> 4)
@@ -252,11 +252,23 @@
             ring_piece(0, way, 0).start()
         pass_on(0, 0, 0).start()
 
-    for first in range(2):
+    def far_weights(first):
         for i in (2 * first, 2 * first + 1):
             arrived(far.at[i], hop2_recv.at[i])
             arrived(far.at[4 + i], hop2_recv.at[4 + i])
         window_pair(far, 1 - win, first)
+
+    far_weights(0)
+
+    @pl.when(active)
+    def _():
+        for d, v in enumerate(ys):
+            arrived(gathered.at[z, v], gy_recv.at[v])
+            for way in range(2):
+                ring_piece(0, way, d + 1).start()
+            pass_on(0, 0, d + 1).start()
+
+    far_weights(1)
 
     lane = lax.broadcasted_iota(jnp.int32, (1, 8, 2 * CH), 2)
     sub = lax.broadcasted_iota(jnp.int32, (1, 8, 2 * CH), 1)
@@ -309,15 +321,9 @@
 
         @pl.when(active)
         def _():
-            if t == 0:
-                for d, v in enumerate(ys):
-                    arrived(gathered.at[z, v], gy_recv.at[v])
-                    for way in range(2):
-                        ring_piece(0, way, d + 1).start()
-                    pass_on(0, 0, d + 1).start()
-            else:
-                if t == 1:
-                    receive(t, 0)
+            if t == 1:
+                receive(t, 0)
+            if t > 0:
                 receive(t, 1)
 
         @pl.when(win != core)

time: 69.6 us -> 69.2 us (level)
  no operation moved by 1% of the time
where the time goes in v8:
time: 69.2 us; the launch traced here: 69.1 us
  Pallas kernels  69.1 us (100%)
    pallas_call x1, Pallas kernels, spread(): pl.pallas_call(spread_kernel, out_shape=jax.ShapeDtypeStruct((2, NY, NZ,...  61.8 us
    pallas_call x1, Pallas kernels, lags(): pl.pallas_call(lag_kernel, out_shape=jax.ShapeDtypeStruct((2, HALF, CH, L...  7.28 us

profile of v8, /device:TPU:1, one launch (start us, length us, event | category | flops | bytes accessed | tf_op | source)
XLA Modules:
  0.0 69.1 jit_solution(10104702744776589194)
XLA Ops:
  0.0 0.0 copy-start
  0.0 0.0 copy-start.1
  0.0 61.8 %shard_map.46 = bf16[2,4,8,512,256]{4,3,2,1,0:T(8,128)(2,1)S(1)} custom-call(s32[2]{0:T(128)} %plan_hbm.1, bf16[8,2,4,16,512]{4,3,2,1,0:T(8,128)(2,1)} %bitcast.3), custom_call_target="tpu_custom_call" | custom-call | tf_op jit(solution)/shard_map/pallas_call | solution.py:367
  61.8 0.0 copy-done
  61.8 0.0 copy-done.1
  61.8 7.3 %shard_map.47 = bf16[2,64,128,256]{3,2,1,0:T(8,128)(2,1)} custom-call(bf16[2,32,512,256]{3,2,1,0:T(8,128)(2,1)S(1)} %bitcast.2, s32[2,64,128]{2,1,0:T(8,128)S(1)} %copy-done.1, bf16[256,512]{1,0:T(8,128)(2,1)S(1)} %copy-done), custom_call_target="tpu_custom_call" | custom-call | tf_op jit(solution)/shard_map/pallas_call | solution.py:441
Async XLA Ops:
  0.0 61.8 %copy-start = (bf16[256,512]{1,0:T(8,128)(2,1)S(1)}, bf16[256,512]{1,0:T(8,128)(2,1)}, u32[]{:S(2)}) copy-start(bf16[256,512]{1,0:T(8,128)(2,1)} %constant.2.clone.table_ref) | copy-start | bytes 786436
  0.0 61.8 %copy-start.1 = (s32[2,64,128]{2,1,0:T(8,128)S(1)}, s32[2,64,128]{2,1,0:T(8,128)}, u32[]{:S(2)}) copy-start(s32[2,64,128]{2,1,0:T(8,128)} %mask_ref.1) | copy-start | bytes 196612

commit v9 on v8

--- a/solution.py
+++ b/solution.py
@@ -285,28 +285,29 @@
         if part != 1:
             lax.fori_loop(0, NY, unpack, 0)
 
-        def product(g):
-            row = sources[:count, :, :, :, pl.ds(g, 1), :].reshape(count * 16, 1, 2 * CH)
+        def product(g, row):
             spread = jnp.where(diagonal, row, 0.0)
             spread = spread.reshape(count * 16 * 8, 2 * CH).astype(jnp.bfloat16)
             res = jnp.dot(spread, weights[g], preferred_element_type=jnp.float32)
             return res.reshape(count * 16, 8, 2 * CH)
 
-        def bins(gg, carry):
-            res = jnp.concatenate([product(2 * gg), product(2 * gg + 1)], 1)
-            res = res.astype(jnp.bfloat16).reshape(count, NY, 2, 2, 16, 2 * CH)
-            row = pl.multiple_of(gg * 16, 16)
-            for i, slot in enumerate(slots):
-                for b in range(2):
-                    for c in range(2):
-                        for s in range(2):
-                            cross[b, :, slot, pl.ds(c * NF + row, 16), s * CH : (s + 1) * CH] = res[
-                                i, :, b, s, :, c * CH : (c + 1) * CH
-                            ]
+        def bins(block, carry):
+            start = pl.multiple_of(8 * block, 8)
+            rows = sources[:count, :, :, :, pl.ds(start, 8), :].reshape(count * 16, 8, 2 * CH)
+            for k in range(0, 8, 2):
+                res = jnp.concatenate([product(start + k + m, rows[:, k + m : k + m + 1]) for m in range(2)], 1)
+                res = res.astype(jnp.bfloat16).reshape(count, NY, 2, 2, 16, 2 * CH)
+                row = pl.multiple_of(block * 64 + 8 * k, 16)
+                for i, slot in enumerate(slots):
+                    for b in range(2):
+                        for c in range(2):
+                            for s in range(2):
+                                cross[b, :, slot, pl.ds(c * NF + row, 16), s * CH : (s + 1) * CH] = res[
+                                    i, :, b, s, :, c * CH : (c + 1) * CH
+                                ]
             return carry
 
-        quarter = GROUPS // 4
-        lax.fori_loop(quarter if part == 1 else 0, quarter if part == 0 else 2 * quarter, bins, 0, unroll=8)
+        lax.fori_loop(2 if part == 1 else 0, 2 if part == 0 else 4, bins, 0)
 
     def receive(t, late):
         for way, d in pieces(t - 1):

time: 69.2 us -> 69.8 us (level)
  no operation moved by 1% of the time
where the time goes in v9:
time: 69.8 us; the launch traced here: 69.7 us
  Pallas kernels  69.7 us (100%)
    pallas_call x1, Pallas kernels, spread(): pl.pallas_call(spread_kernel, out_shape=jax.ShapeDtypeStruct((2, NY, NZ,...  62.4 us
    pallas_call x1, Pallas kernels, lags(): pl.pallas_call(lag_kernel, out_shape=jax.ShapeDtypeStruct((2, HALF, CH, L...  7.27 us

profile of v9, /device:TPU:1, one launch (start us, length us, event | category | flops | bytes accessed | tf_op | source)
XLA Modules:
  0.0 69.7 jit_solution(18326075060980339180)
XLA Ops:
  0.0 0.0 copy-start
  0.0 0.0 copy-start.1
  0.0 62.4 %shard_map.46 = bf16[2,4,8,512,256]{4,3,2,1,0:T(8,128)(2,1)S(1)} custom-call(s32[2]{0:T(128)} %plan_hbm.1, bf16[8,2,4,16,512]{4,3,2,1,0:T(8,128)(2,1)} %bitcast.3), custom_call_target="tpu_custom_call" | custom-call | tf_op jit(solution)/shard_map/pallas_call | solution.py:368
  62.4 0.0 copy-done
  62.4 0.0 copy-done.1
  62.5 7.3 %shard_map.47 = bf16[2,64,128,256]{3,2,1,0:T(8,128)(2,1)} custom-call(bf16[2,32,512,256]{3,2,1,0:T(8,128)(2,1)S(1)} %bitcast.2, s32[2,64,128]{2,1,0:T(8,128)S(1)} %copy-done.1, bf16[256,512]{1,0:T(8,128)(2,1)S(1)} %copy-done), custom_call_target="tpu_custom_call" | custom-call | tf_op jit(solution)/shard_map/pallas_call | solution.py:442
Async XLA Ops:
  0.0 62.4 %copy-start = (bf16[256,512]{1,0:T(8,128)(2,1)S(1)}, bf16[256,512]{1,0:T(8,128)(2,1)}, u32[]{:S(2)}) copy-start(bf16[256,512]{1,0:T(8,128)(2,1)} %constant.2.clone.table_ref) | copy-start | bytes 786436
  0.0 62.4 %copy-start.1 = (s32[2,64,128]{2,1,0:T(8,128)S(1)}, s32[2,64,128]{2,1,0:T(8,128)}, u32[]{:S(2)}) copy-start(s32[2,64,128]{2,1,0:T(8,128)} %mask_ref.1) | copy-start | bytes 196612

commit v10 on v7

--- a/solution.py
+++ b/solution.py
@@ -213,7 +213,7 @@
         return (z + t) % NZ
 
     def pieces(t):
-        return [(0, 0), (0, 1), (1, 2), (1, 3)] if t == 3 else [(way, d) for d in range(NY) for way in range(2)]
+        return [(0, 0), (0, 1), (1, 3), (1, 2)] if t == 3 else [(way, d) for d in (0, 1, 3, 2) for way in range(2)]
 
     def piece(t, way, d):
         return gathered.at[down(t) if way == 0 else up(t), (y + d) % NY]
@@ -228,7 +228,7 @@
         return remote(ref, ref, gc_send.at[slot, d], gc_recv.at[slot, d], at(core_=1 - core))
 
     def passed(t):
-        return [(0, d) for d in range(NY)] if t in (0, 4) else [(way, d) for d in range(NY) for way in range(2)]
+        return [(0, d) for d in (0, 1, 3, 2)] if t in (0, 4) else [(way, d) for d in (0, 1, 3, 2) for way in range(2)]
 
     own = gathered.at[z, y]
 
@@ -310,11 +310,11 @@
         @pl.when(active)
         def _():
             if t == 0:
-                for d, v in enumerate(ys):
-                    arrived(gathered.at[z, v], gy_recv.at[v])
+                for d in (1, 3, 2):
+                    arrived(piece(0, 0, d), gy_recv.at[(y + d) % NY])
                     for way in range(2):
-                        ring_piece(0, way, d + 1).start()
-                    pass_on(0, 0, d + 1).start()
+                        ring_piece(0, way, d).start()
+                    pass_on(0, 0, d).start()
             else:
                 if t == 1:
                     receive(t, 0)

time: 69.6 us -> 69 us (level)
  no operation moved by 1% of the time
where the time goes in v10:
time: 69 us
  Pallas kernels  68.9 us (100%)
    pallas_call x1, Pallas kernels, spread(): pl.pallas_call(spread_kernel, out_shape=jax.ShapeDtypeStruct((2, NY, NZ,...  61.6 us
    pallas_call x1, Pallas kernels, lags(): pl.pallas_call(lag_kernel, out_shape=jax.ShapeDtypeStruct((2, HALF, CH, L...  7.27 us

profile of v10, /device:TPU:1, one launch (start us, length us, event | category | flops | bytes accessed | tf_op | source)
XLA Modules:
  0.0 69.0 jit_solution(1429353127985029175)
XLA Ops:
  0.0 0.0 copy-start
  0.0 0.0 copy-start.1
  0.0 61.6 %shard_map.46 = bf16[2,4,8,512,256]{4,3,2,1,0:T(8,128)(2,1)S(1)} custom-call(s32[2]{0:T(128)} %plan_hbm.1, bf16[8,2,4,16,512]{4,3,2,1,0:T(8,128)(2,1)} %bitcast.3), custom_call_target="tpu_custom_call" | custom-call | tf_op jit(solution)/shard_map/pallas_call | solution.py:361
  61.7 0.0 copy-done
  61.7 0.0 copy-done.1
  61.7 7.3 %shard_map.47 = bf16[2,64,128,256]{3,2,1,0:T(8,128)(2,1)} custom-call(bf16[2,32,512,256]{3,2,1,0:T(8,128)(2,1)S(1)} %bitcast.2, s32[2,64,128]{2,1,0:T(8,128)S(1)} %copy-done.1, bf16[256,512]{1,0:T(8,128)(2,1)S(1)} %copy-done), custom_call_target="tpu_custom_call" | custom-call | tf_op jit(solution)/shard_map/pallas_call | solution.py:435
Async XLA Ops:
  0.0 61.7 %copy-start = (bf16[256,512]{1,0:T(8,128)(2,1)S(1)}, bf16[256,512]{1,0:T(8,128)(2,1)}, u32[]{:S(2)}) copy-start(bf16[256,512]{1,0:T(8,128)(2,1)} %constant.2.clone.table_ref) | copy-start | bytes 786436
  0.0 61.7 %copy-start.1 = (s32[2,64,128]{2,1,0:T(8,128)S(1)}, s32[2,64,128]{2,1,0:T(8,128)}, u32[]{:S(2)}) copy-start(s32[2,64,128]{2,1,0:T(8,128)} %mask_ref.1) | copy-start | bytes 196612

commit v11 on v10

--- a/solution.py
+++ b/solution.py
@@ -18,7 +18,7 @@
 GROUPS = 32
 MESH = pl.DeviceIdType.MESH
 NY, NZ = 4, 8
-BATCH = 16
+BATCH = 32
 BUFFERS = 2 * BATCH
 
 
@@ -294,7 +294,7 @@
             return carry
 
         quarter = GROUPS // 4
-        lax.fori_loop(quarter if part == 1 else 0, quarter if part == 0 else 2 * quarter, bins, 0, unroll=8)
+        lax.fori_loop(quarter if part == 1 else 0, quarter if part == 0 else 2 * quarter, bins, 0, unroll=4)
 
     def receive(t, late):
         for way, d in pieces(t - 1):

time: 69 us -> 69.8 us (1.012)
  Pallas kernels: 68.9 us -> 69.7 us
where the time goes in v11:
time: 69.8 us; the launch traced here: 69.7 us
  Pallas kernels  69.7 us (100%)
    pallas_call x1, Pallas kernels, spread(): pl.pallas_call(spread_kernel, out_shape=jax.ShapeDtypeStruct((2, NY, NZ,...  62.2 us
    pallas_call x1, Pallas kernels, lags(): pl.pallas_call(lag_kernel, out_shape=jax.ShapeDtypeStruct((2, HALF, CH, L...  7.52 us

profile of v11, /device:TPU:1, one launch (start us, length us, event | category | flops | bytes accessed | tf_op | source)
XLA Modules:
  0.0 69.7 jit_solution(17549067782264785350)
XLA Ops:
  0.0 0.0 copy-start
  0.0 0.0 copy-start.1
  0.0 62.2 %shard_map.46 = bf16[2,4,8,512,256]{4,3,2,1,0:T(8,128)(2,1)S(1)} custom-call(s32[2]{0:T(128)} %plan_hbm.1, bf16[8,2,4,16,512]{4,3,2,1,0:T(8,128)(2,1)} %bitcast.3), custom_call_target="tpu_custom_call" | custom-call | tf_op jit(solution)/shard_map/pallas_call | solution.py:361
  62.2 0.0 copy-done
  62.2 0.0 copy-done.1
  62.2 7.5 %shard_map.47 = bf16[2,64,128,256]{3,2,1,0:T(8,128)(2,1)} custom-call(bf16[2,32,512,256]{3,2,1,0:T(8,128)(2,1)S(1)} %bitcast.2, s32[2,64,128]{2,1,0:T(8,128)S(1)} %copy-done.1, bf16[256,512]{1,0:T(8,128)(2,1)S(1)} %copy-done), custom_call_target="tpu_custom_call" | custom-call | tf_op jit(solution)/shard_map/pallas_call | solution.py:435
Async XLA Ops:
  0.0 62.2 %copy-start = (bf16[256,512]{1,0:T(8,128)(2,1)S(1)}, bf16[256,512]{1,0:T(8,128)(2,1)}, u32[]{:S(2)}) copy-start(bf16[256,512]{1,0:T(8,128)(2,1)} %constant.2.clone.table_ref) | copy-start | bytes 786436
  0.0 62.2 %copy-start.1 = (s32[2,64,128]{2,1,0:T(8,128)S(1)}, s32[2,64,128]{2,1,0:T(8,128)}, u32[]{:S(2)}) copy-start(s32[2,64,128]{2,1,0:T(8,128)} %mask_ref.1) | copy-start | bytes 196612
